TPU v7x, 32 devices: a whole 2x2x4 slice. The times are simulated.
32 devices in a mesh: groups: 2 (over x), dp: 16 (over z, y, core).
Axes of the slice: x: 2, y: 2, z: 4, core: 2. Of those that a mesh axis runs over, the one named last changes fastest.
Arguments:
- train_inputs: bfloat16 [8192, 4096], P(('groups', 'dp')), parts along dimension 0, may hold values from -4000 to 4000
- train_grads: bfloat16 [8192, 14336], P(('groups', 'dp')), parts along dimension 0, may hold values from -4000 to 4000
- proj_in: bfloat16 [64, 4096], replicated, may hold values from -0.09375 to 0.09375
- proj_out: bfloat16 [64, 14336], replicated, may hold values from -0.046875 to 0.046875
- query_grads: bfloat16 [256, 4096], P(('groups', 'dp')), parts along dimension 0, may hold values from -6 to 6
Outputs:
- scores: float32 [32, 128], P(('groups', 'dp')), parts along dimension 0
There are 2 independent parts, one for each index of `groups`. A program takes and returns all parts, laid end to end along the dimension named above; an argument that names none is the same for every part. Nothing has to cross between parts.
All inputs are finite; a program needn't handle non-finite values.
Results may differ from a plain program's by a relative error of at most 0.0003.
Values may be sent and summed in bfloat16 or wider, within the bound.
No kernel may reach another device: no remote copies, remote signals or barrier semaphores. Data moves between devices by JAX's collectives and lax.ppermute only.
A program may use at most 128 MiB of HBM per device.

v0:
```python
import jax
import jax.numpy as jnp
from jax import lax
from jax.sharding import PartitionSpec as P

SEQ = 256


def project_rows(token_rows, weight):
    return lax.dot_general(
        token_rows, weight, (((1,), (1,)), ((), ())), preferred_element_type=jnp.float32
    )


def damped_inverse(moment):
    rank_size = moment.shape[0]
    identity = jnp.eye(rank_size, dtype=jnp.float32)
    damped = moment + 0.1 * jnp.trace(moment) / rank_size * identity
    factor = jnp.linalg.cholesky(damped)
    return jax.scipy.linalg.cho_solve((factor, True), identity)


def precondition(matrices, left_side, right_side):
    rank_size = left_side.shape[0]
    stacked = matrices.astype(jnp.float32).reshape(-1, rank_size, rank_size)
    result = jnp.einsum(
        "ab,kbc,cd->kad", left_side, stacked, right_side, precision=lax.Precision.HIGHEST
    )
    return result.reshape(-1, rank_size * rank_size)


def inner_rows(left_rows, right_rows):
    return jnp.dot(left_rows, right_rows.astype(jnp.float32).T, precision=lax.Precision.HIGHEST)


def body(train_inputs, train_grads, proj_in, proj_out, query_grads):
    rank_size = proj_in.shape[0]
    examples_count = train_inputs.shape[0] // SEQ
    inputs_low = project_rows(train_inputs, proj_in)
    grads_low = project_rows(train_grads, proj_out)
    outer = jnp.einsum(
        "esa,esb->eab",
        grads_low.reshape(examples_count, SEQ, rank_size),
        inputs_low.reshape(examples_count, SEQ, rank_size),
        precision=lax.Precision.HIGHEST,
    )
    examples = outer.reshape(examples_count, rank_size * rank_size)
    local_in = jnp.dot(inputs_low.T, inputs_low, precision=lax.Precision.HIGHEST)
    local_out = jnp.dot(grads_low.T, grads_low, precision=lax.Precision.HIGHEST)
    summed_in, summed_out = lax.psum((local_in, local_out), "dp")
    token_total = train_inputs.shape[0] * lax.axis_size("dp")
    inverse_in = damped_inverse(summed_in / token_total)
    inverse_out = damped_inverse(summed_out / token_total)
    scores = inner_rows(
        examples,
        precondition(
            lax.all_gather(query_grads, "dp", axis=0, tiled=True), inverse_out, inverse_in
        ),
    )
    return scores / rank_size


def solution(mesh):
    return jax.shard_map(
        body,
        mesh=mesh,
        in_specs=(
            P(("groups", "dp"), None),
            P(("groups", "dp"), None),
            P(),
            P(),
            P(("groups", "dp"), None),
        ),
        out_specs=P(("groups", "dp"), None),
        check_vma=False,
    )
```

profile of v0, /device:TPU:0, one launch (start us, length us, event | category | flops | bytes accessed | tf_op | source)
XLA Modules:
  0.0 136.8 jit_solution(12776995912005568117)
XLA Ops:
  6.5 0.0 copy-start
  6.5 0.0 all-gather.2.cloned.1.call-start
  6.5 0.7 all-gather.2.cloned.1.call-update
  7.3 0.9 copy-done
  8.1 1.8 %fusion.25 = f32[256,64]{0,1:T(8,128)S(1)} fusion(bf16[256,4096]{1,0:T(8,128)(2,1)S(1)} %copy-done, bf16[64,4096]{1,0:T(8,128)(2,1)} %param.10), kind=kOutput, calls=%fused_computation.37 | convolution fusion | flops 134217728 | bytes 2686976 | tf_op jit(solution)/shard_map/dot_general | solution.py:10
  9.9 0.2 fusion.28
  10.1 6.0 %fusion.24 = f32[256,64]{0,1:T(8,128)S(1)} fusion(bf16[256,14336]{1,0:T(8,128)(2,1)} %param.9, bf16[64,14336]{1,0:T(8,128)(2,1)} %param.11), kind=kOutput, calls=%fused_computation.36 | convolution fusion | flops 469762048 | bytes 9240576 | tf_op jit(solution)/shard_map/dot_general | solution.py:10
  16.1 0.2 fusion.27
  16.3 63.2 %all-reduce = (f32[64,64]{0,1:T(8,128)S(1)}, f32[64,64]{0,1:T(8,128)S(1)}) all-reduce(f32[64,64]{0,1:T(8,128)S(1)} %fusion.27, f32[64,64]{0,1:T(8,128)S(1)} %fusion.28), channel_id=1, replica_groups=mesh['groups'=2,'dp'=16] {'dp'}, use_global_device_ids=true, to_apply=%region_0.0 | all-reduce | flops 8192 | bytes 65536 | tf_op jit(solution)/shard_map/psum | solution.py:50
  79.5 0.6 select_reduce_fusion.2
  80.1 0.7 select_reduce_fusion.3
  82.2 0.1 copy.20
  82.3 5.8 %cholesky.55 = f32[64,64]{1,0:T(8,128)S(1)} custom-call(f32[64,64]{1,0:T(8,128)S(1)} %fusion.20), custom_call_target="Cholesky" | custom-call | tf_op jit(solution)/shard_map/jit(cholesky)/cholesky | solution.py:19
  88.2 0.6 compare_reduce_fusion
  88.8 0.7 fusion.17
  89.5 4.9 %custom-call.9 = f32[1,64,64]{1,2,0:T(8,128)S(1)} custom-call(f32[1,64,64]{2,1,0:T(8,128)S(1)} %fusion.17), custom_call_target="InvertDiagBlocksLowerTriangular" | custom-call | tf_op jit(solution)/shard_map/jit(_cho_solve)/triangular_solve | solution.py:20
  94.4 0.1 copy.16
  94.5 5.8 %cholesky.44 = f32[64,64]{1,0:T(8,128)S(1)} custom-call(f32[64,64]{1,0:T(8,128)S(1)} %fusion.23), custom_call_target="Cholesky" | custom-call | tf_op jit(solution)/shard_map/jit(cholesky)/cholesky | solution.py:19
  100.3 0.6 compare_reduce_fusion.1
  101.0 0.7 fusion.16
  101.6 4.9 %custom-call.8 = f32[1,64,64]{1,2,0:T(8,128)S(1)} custom-call(f32[1,64,64]{2,1,0:T(8,128)S(1)} %fusion.16), custom_call_target="InvertDiagBlocksLowerTriangular" | custom-call | tf_op jit(solution)/shard_map/jit(_cho_solve)/triangular_solve | solution.py:20
  106.5 0.2 fusion.12
  106.8 0.2 convolution_bitcast_fusion.1
  107.0 0.2 fusion.14
  107.2 0.2 convolution_bitcast_fusion.2
  107.4 0.2 fusion.26
  107.6 0.0 all-gather.2.cloned.1.call-done
  107.6 1.6 %copy.17 = bf16[128,4096]{0,1:T(8,128)(2,1)S(1)} copy(bf16[128,4096]{1,0:T(8,128)(2,1)} %all-gather.2.cloned.1.call-done) | data formatting | bytes 2097152 | tf_op jit(solution)/shard_map/all_gather | solution.py:57
  109.2 2.7 %convolution_bitcast_fusion = f32[128,64,64]{0,2,1:T(8,128)} fusion(f32[64,64,1]{1,0,2:T(8,128)S(1)} %convolution_bitcast_fusion.2, bf16[128,64,64]{0,2,1:T(8,128)(2,1)S(1)} %bitcast.56), kind=kOutput, calls=%fused_computation.2 | convolution fusion | flops 402653184 | bytes 3162112 | tf_op jit(solution)/shard_map/ab,kbc,cd->kad/dot_general | solution.py:26
  112.0 5.6 %copy.21 = f32[128,64,64]{1,2,0:T(8,128)} copy(f32[128,64,64]{0,2,1:T(8,128)} %convolution_bitcast_fusion) | data formatting | bytes 4194304 | tf_op jit(solution)/shard_map/ab,kbc,cd->kad/dot_general | solution.py:26
  117.6 6.7 %fusion.29 = f32[128,64,64]{2,1,0:T(8,128)S(1)} fusion(f32[128,64,64]{1,2,0:T(8,128)} %copy.21, f32[64,64,1]{1,0,2:T(8,128)S(1)} %convolution_bitcast_fusion.1), kind=kOutput, calls=%fused_computation.41 | convolution fusion | flops 402653184 | bytes 4210688 | tf_op jit(solution)/shard_map/ab,kbc,cd->kad/dot_general | solution.py:26
  124.3 5.7 %fusion.8 = f32[1,128]{1,0:T(1,128)} fusion(f32[64,64,1]{1,2,0:T(1,128)S(1)} %bitcast.57, f32[128,64,64]{2,1,0:T(8,128)S(1)} %fusion.29), kind=kOutput, calls=%fused_computation.7 | convolution fusion | flops 6291584 | bytes 2114048 | tf_op jit(solution)/shard_map/dot_general | solution.py:33
  (5 shorter events, 0.1 us)
Async XLA Ops:
  6.5 1.6 %copy-start = (bf16[256,4096]{1,0:T(8,128)(2,1)S(1)}, bf16[256,4096]{1,0:T(8,128)(2,1)}, u32[]{:S(2)}) copy-start(bf16[256,4096]{1,0:T(8,128)(2,1)} %param.8) | copy-start | bytes 6291460
  6.5 101.1 %all-gather.2.cloned.1.call-start = ((), (), s32[]{:S(2)}) async-start(), calls=%async_computation | async-start | bytes 1114112 | tf_op jit(solution)/shard_map/all_gather | solution.py:57
Sparse Core Ops, SparseCore 0:
  9.5 40.7 all-gather.1
where the time goes:
time: 137 us
  blocking collectives  63.2 us (46%)
  other arithmetic  25.5 us (19%)
  matrix products  24.3 us (18%)
  between operations  14.9 us (11%)
  local copies, waits for them, and re-layouts  8.26 us (6%)
    psum x1, blocking collectives, body(): summed_in, summed_out = lax.psum((local_in, local_out), 'dp')  63.2 us
    another operation x6, other arithmetic, damped_inverse(): factor = jnp.linalg.cholesky(damped)  13 us
    another operation x4, other arithmetic, damped_inverse(): return jax.scipy.linalg.cho_solve((factor, True), identity)  11.1 us
    dot_general x2, matrix products, precondition(): jnp.einsum('ab,kbc,cd->kad', left_side, stacked, right_side, precision=la...  9.41 us
    dot_general x2, matrix products, project_rows(): lax.dot_general(token_rows, weight, (((1,), (1,)), ((), ())), preferred_e...  7.78 us
    dot_general x1, matrix products, inner_rows(): jnp.dot(left_rows, right_rows.astype(jnp.float32).T, precision=lax.Precis...  5.7 us
    dot_general x1, local copies, waits for them, and re-layouts, precondition(): jnp.einsum('ab,kbc,cd->kad', left_side, stacked, right_side, precision=la...  5.61 us
  transfers between devices with their start and end apart: 1, of which 0 were waited for; matrix products, arithmetic and copies ran while one was open for 25% of the time, Pallas kernels for 0%

commit v1 on v0

v1 whole, which is shorter than its diff:
```python
import functools

import jax
import jax.numpy as jnp
from jax import lax
from jax.experimental import pallas as pl
from jax.experimental.pallas import tpu as pltpu
from jax.sharding import PartitionSpec as P

SEQ = 256
DAMPING = 0.1
CHUNK = 2048
MIB = 1024 * 1024
HIGHEST = lax.Precision.HIGHEST


def project_kernel(rank, plan, x_hbm, g_hbm, pin_hbm, pout_hbm, m_ref, e_ref, tok, wts, sems):
    copies = []
    for k, (which, start, size) in enumerate(plan):
        src, w_src = ((x_hbm, pin_hbm), (g_hbm, pout_hbm))[which]
        copies.append((
            pltpu.make_async_copy(w_src.at[:, pl.ds(start, size)], wts.at[k, :, pl.ds(0, size)], sems.at[0, k]),
            pltpu.make_async_copy(src.at[:, pl.ds(start, size)], tok.at[k, :, pl.ds(0, size)], sems.at[1, k]),
        ))
    for pair in copies:
        for copy in pair:
            copy.start()
    low = [None, None]
    for k, (which, start, size) in enumerate(plan):
        for copy in copies[k]:
            copy.wait()
        part = lax.dot_general(
            tok[k, :, :size], wts[k, :, :size], (((1,), (1,)), ((), ())), preferred_element_type=jnp.float32
        )
        low[which] = part if low[which] is None else low[which] + part
    both = jnp.concatenate(low, axis=1)
    gram = lax.dot_general(
        both, both, (((0,), (0,)), ((), ())), precision=HIGHEST, preferred_element_type=jnp.float32
    )
    lane = lax.broadcasted_iota(jnp.int32, (rank, 2 * rank), 1)
    m_ref[...] = jnp.where(lane < rank, gram[:rank], gram[rank:])
    e_ref[...] = gram[rank:]


def project(x, g, proj_in, proj_out):
    rank = proj_in.shape[0]
    plan = []
    for which, width in ((0, x.shape[1]), (1, g.shape[1])):
        for start in range(0, width, CHUNK):
            plan.append((which, start, min(CHUNK, width - start)))
    rows = x.shape[0]
    out = jax.ShapeDtypeStruct((rank, 2 * rank), jnp.float32)
    return pl.pallas_call(
        functools.partial(project_kernel, rank, plan),
        out_shape=(out, out),
        in_specs=[pl.BlockSpec(memory_space=pl.ANY)] * 4,
        out_specs=(pl.BlockSpec(memory_space=pltpu.VMEM),) * 2,
        scratch_shapes=[
            pltpu.VMEM((len(plan), rows, CHUNK), x.dtype),
            pltpu.VMEM((len(plan), rank, CHUNK), x.dtype),
            pltpu.SemaphoreType.DMA((2, len(plan))),
        ],
        compiler_params=pltpu.CompilerParams(vmem_limit_bytes=24 * MIB),
        cost_estimate=pl.CostEstimate(
            flops=2 * rows * rank * (x.shape[1] + g.shape[1]),
            bytes_accessed=2 * (rows + rank) * (x.shape[1] + g.shape[1]),
            transcendentals=0,
        ),
        name="project",
    )(x, g, proj_in, proj_out)


def newton_scales(rank):
    low = 2.0 / (2.0 + rank / DAMPING)
    scales = []
    while 1.0 - low > 0.02:
        image = low * (2.0 - low)
        scale = 2.0 / (1.0 + image)
        scales.append(scale)
        low = scale * image
    return scales


def dot(a, b):
    return jnp.dot(a, b, precision=HIGHEST, preferred_element_type=jnp.float32)


def score_kernel(rank, tokens, slots, m_ref, mr_ref, e_ref, qa_ref, qb_ref, o_ref, rows_scr, acc_scr):
    size = 2 * rank
    me = lax.axis_index("dp")
    total = (m_ref[...] + mr_ref[...]) * (1.0 / tokens)
    row = lax.broadcasted_iota(jnp.int32, (size, size), 0)
    col = lax.broadcasted_iota(jnp.int32, (size, size), 1)
    same = (row < rank) == (col < rank)
    eye = jnp.where(row == col, 1.0, 0.0)
    moment = jnp.where(same, jnp.concatenate([total, total], axis=0), 0.0)
    diagonal = jnp.where(row == col, moment, 0.0)
    by_col = jnp.sum(diagonal, axis=0, keepdims=True)
    half = lax.broadcasted_iota(jnp.int32, (1, size), 1) < rank
    trace_in = jnp.sum(jnp.where(half, by_col, 0.0), axis=1, keepdims=True)
    trace_out = jnp.sum(jnp.where(half, 0.0, by_col), axis=1, keepdims=True)
    damp = jnp.where(half, trace_in, trace_out) * (DAMPING / rank)
    a = moment + eye * damp
    first = (2.0 / (2.0 + rank / DAMPING)) / damp
    t = a * first
    x = eye * first
    for step, scale in enumerate(newton_scales(rank)):
        turn = 2.0 * eye - t
        x = scale * (x * turn if step == 0 else dot(x, turn))
        if step == 0:
            x = scale * (turn * first)
        t = scale * dot(t, turn)
    x = x + dot(x, eye - t)
    for _ in range(2):
        x = x + dot(x, eye - dot(a, x))
    pre = dot(dot(x[rank:, rank:], e_ref[:, :rank]), x[:rank, :])
    rows_scr[...] = pre
    even = rows_scr[pl.ds(0, rank // 2, stride=2), :]
    odd = rows_scr[pl.ds(1, rank // 2, stride=2), :]
    lane = lax.broadcasted_iota(jnp.int32, (rank // 2, size), 1)
    flat = jnp.where(lane < rank, even, pltpu.roll(odd, rank, 1))
    count = qa_ref.shape[0] // 16
    each = qa_ref.shape[0] * 2 // len(slots)
    for part, q_ref in enumerate((qa_ref, qb_ref)):
        for i in range(count):
            acc = jnp.zeros((16, size), jnp.float32)
            for j in range(rank // 2):
                block = q_ref[pl.ds(16 * i, 16), pl.ds(j * size, size)].astype(jnp.float32)
                acc = acc + block * flat[j:j + 1, :]
            for h in range(2):
                slot = slots[part * 2 * count + 2 * i + h]
                acc_scr[pl.ds(pl.multiple_of((me ^ slot) * each, each), each), :] = acc[8 * h:8 * h + 8]
    ones = jnp.ones((8, size), jnp.float32)
    sums = lax.dot_general(
        ones, acc_scr[...], (((1,), (1,)), ((), ())), precision=HIGHEST, preferred_element_type=jnp.float32
    )
    o_ref[...] = sums[0:1] * (1.0 / rank)


def body(n, train_inputs, train_grads, proj_in, proj_out, query_grads):
    rank = proj_in.shape[0]
    steps = [1 << b for b in range(n.bit_length() - 1)]

    def swap(value, step):
        return lax.ppermute(value, "dp", [(i, i ^ step) for i in range(n)])

    queries, slots = query_grads, [0]
    for step in reversed(steps):
        received = swap(queries, step)
        slots = slots + [slot ^ step for slot in slots]
        if step > 1:
            queries = jnp.concatenate([queries, received], axis=0)
    moment, example = project(train_inputs, train_grads, proj_in, proj_out)
    order = steps[:1] + steps[:0:-1]
    for step in order[:-1]:
        moment = moment + swap(moment, step)
    moment_far = swap(moment, order[-1])
    count = query_grads.shape[0] * n
    return pl.pallas_call(
        functools.partial(score_kernel, rank, train_inputs.shape[0] * n, slots),
        out_shape=jax.ShapeDtypeStruct((1, count), jnp.float32),
        in_specs=[pl.BlockSpec(memory_space=pltpu.VMEM)] * 5,
        out_specs=pl.BlockSpec(memory_space=pltpu.VMEM),
        scratch_shapes=[
            pltpu.VMEM((rank, 2 * rank), jnp.float32),
            pltpu.VMEM((count, 2 * rank), jnp.float32),
        ],
        compiler_params=pltpu.CompilerParams(vmem_limit_bytes=24 * MIB),
        name="score",
    )(moment, moment_far, example, queries, received)


def solution(mesh):
    n = mesh.shape["dp"]
    return jax.shard_map(
        functools.partial(body, n),
        mesh=mesh,
        in_specs=(
            P(("groups", "dp"), None),
            P(("groups", "dp"), None),
            P(),
            P(),
            P(("groups", "dp"), None),
        ),
        out_specs=P(("groups", "dp"), None),
        check_vma=False,
    )
```

time: 137 us -> 53.3 us (0.39)
  blocking collectives: 63.2 us -> 0 us
  matrix products: 24.3 us -> 0 us
  other arithmetic: 25.5 us -> 1.72 us
  waiting for transfers between devices: 0.73 us -> 19.6 us
  between operations: 14.9 us -> 0.06 us
  starting transfers between devices: 0.01 us -> 13.4 us
  Pallas kernels: 0 us -> 11.1 us
    psum x1 -> x0, blocking collectives: 63.2 us -> none  [body(): summed_in, summed_out = lax.psum((local_in, local_out), 'dp')]
    another operation x10 -> x0, other arithmetic: 24.1 us -> none  [the longest x6 13 us: damped_inverse(): factor = jnp.linalg.cholesky(damped)]
    dot_general x8 -> x0, matrix products: 23.5 us -> none  [the longest x2 9.41 us: precondition(): jnp.einsum('ab,kbc,cd->kad', left_side, stacked, right_side, precision=la...]
    ppermute x0 -> x8, waiting for transfers between devices: none -> 19.6 us  [swap(): return lax.ppermute(value, 'dp', [(i, i ^ step) for i in range(n)])]
    ppermute x0 -> x8, starting transfers between devices: none -> 13.4 us  [swap(): return lax.ppermute(value, 'dp', [(i, i ^ step) for i in range(n)])]
    pallas_call x0 -> x2, Pallas kernels: none -> 11.1 us  [the longest x1 7.02 us: project(): pl.pallas_call(functools.partial(project_kernel, rank, plan), out_shape=(...]
    unnamed x2 -> x11, local copies, waits for them, and re-layouts: 0.87 us -> 7.06 us
    dot_general x1 -> x0, local copies, waits for them, and re-layouts: 5.61 us -> none  [precondition(): jnp.einsum('ab,kbc,cd->kad', left_side, stacked, right_side, precision=la...]
  transfers between devices with their start and end apart: 1 -> 8, of which waited for: 0 -> 7; matrix products, arithmetic and copies ran while one was open for 25% -> 2% of each run, Pallas kernels for 0% -> 13%
where the time goes in v1:
time: 53.3 us; the launch traced here: 52.9 us
  waiting for transfers between devices  19.6 us (37%)
  starting transfers between devices  13.4 us (25%)
  Pallas kernels  11.1 us (21%)
  local copies, waits for them, and re-layouts  7.08 us (13%)
  other arithmetic  1.72 us (3%)
    ppermute x8, waiting for transfers between devices, swap(): return lax.ppermute(value, 'dp', [(i, i ^ step) for i in range(n)])  19.6 us
    ppermute x8, starting transfers between devices, swap(): return lax.ppermute(value, 'dp', [(i, i ^ step) for i in range(n)])  13.4 us
    unnamed x11, local copies, waits for them, and re-layouts  7.06 us
    pallas_call x1, Pallas kernels, project(): pl.pallas_call(functools.partial(project_kernel, rank, plan), out_shape=(...  7.02 us
    pallas_call x1, Pallas kernels, body(): pl.pallas_call(functools.partial(score_kernel, rank, train_inputs.shape[0...  4.12 us
    concatenate x2, other arithmetic, body(): queries = jnp.concatenate([queries, received], axis=0)  1.71 us
  transfers between devices with their start and end apart: 8, of which 7 were waited for; matrix products, arithmetic and copies ran while one was open for 2% of the time, Pallas kernels for 13%

profile of v1, /device:TPU:0, one launch (start us, length us, event | category | flops | bytes accessed | tf_op | source)
XLA Modules:
  0.0 52.9 jit_solution(15025403861330496068)
XLA Ops:
  0.0 0.0 copy-start.3
  0.0 4.0 %collective-permute-start.4 = (bf16[8,4096]{1,0:T(8,128)(2,1)}, bf16[8,4096]{1,0:T(8,128)(2,1)S(1)}, u32[]{:S(2)}, u32[]{:S(2)}) collective-permute-start(bf16[8,4096]{1,0:T(8,128)(2,1)} %param.9), channel_id=1, source_target_pairs={{0,8},{1,9},{2,10},{3,11},{4,12},{5,13},{6,14},{7,15},{8,0},{9,1},... | collective-permute-start | bytes 196616 | tf_op jit(solution)/shard_map/ppermute | solution.py:145
  4.0 0.9 %constant_dynamic-update-slice_fusion.3 = bf16[64,4096]{1,0:T(8,128)(2,1)S(1)} fusion(bf16[8,4096]{1,0:T(8,128)(2,1)} %param.9), kind=kLoop, calls=%fused_computation.5 | loop fusion | bytes 131072
  4.9 3.0 %collective-permute-done.4 = bf16[8,4096]{1,0:T(8,128)(2,1)S(1)} collective-permute-done((bf16[8,4096]{1,0:T(8,128)(2,1)}, bf16[8,4096]{1,0:T(8,128)(2,1)S(1)}, u32[]{:S(2)}, u32[]{:S(2)}) %collective-permute-start.4) | collective-permute-done | bytes 65568 | tf_op jit(solution)/shard_map/ppermute | solution.py:145
  7.9 0.8 %pad_maximum_fusion.1 = bf16[16,4096]{1,0:T(8,128)(2,1)S(1)} fusion(bf16[8,4096]{1,0:T(8,128)(2,1)S(1)} %collective-permute-done.4, bf16[8,4096]{1,0:T(8,128)(2,1)} %param.9), kind=kLoop, calls=%fused_computation.1 | loop fusion | flops 262144 | bytes 262144 | tf_op jit(solution)/shard_map/concatenate | solution.py:152
  8.7 0.7 %collective-permute-start.5 = (bf16[16,4096]{1,0:T(8,128)(2,1)S(1)}, bf16[16,4096]{1,0:T(8,128)(2,1)S(1)}, u32[]{:S(2)}, u32[]{:S(2)}) collective-permute-start(bf16[16,4096]{1,0:T(8,128)(2,1)S(1)} %pad_maximum_fusion.1), channel_id=1, source_target_pairs={{0,4},{1,5},{2,6},{3,7},{4,0},{5,1},{6,2},{7,3},{8,12},{9,13},{10,... | collective-permute-start | bytes 393224 | tf_op jit(solution)/shard_map/ppermute | solution.py:145
  9.5 4.3 %collective-permute-done.5 = bf16[16,4096]{1,0:T(8,128)(2,1)S(1)} collective-permute-done((bf16[16,4096]{1,0:T(8,128)(2,1)S(1)}, bf16[16,4096]{1,0:T(8,128)(2,1)S(1)}, u32[]{:S(2)}, u32[]{:S(2)}) %collective-permute-start.5) | collective-permute-done | bytes 131104 | tf_op jit(solution)/shard_map/ppermute | solution.py:145
  13.8 0.9 %pad_maximum_fusion = bf16[32,4096]{1,0:T(8,128)(2,1)S(1)} fusion(bf16[16,4096]{1,0:T(8,128)(2,1)S(1)} %collective-permute-done.5, bf16[8,4096]{1,0:T(8,128)(2,1)S(1)} %collective-permute-done.4, bf16[8,4096]{1,0:T(8,128)(2,1)} %param.9), kind=kLoop, calls=%fused_computation | loop fusion | flops 786432 | bytes 524288 | tf_op jit(solution)/shard_map/concatenate | solution.py:152
  14.6 1.8 %collective-permute-start.6 = (bf16[32,4096]{1,0:T(8,128)(2,1)S(1)}, bf16[32,4096]{1,0:T(8,128)(2,1)S(1)}, u32[]{:S(2)}, u32[]{:S(2)}) collective-permute-start(bf16[32,4096]{1,0:T(8,128)(2,1)S(1)} %pad_maximum_fusion), channel_id=1, source_target_pairs={{0,2},{1,3},{2,0},{3,1},{4,6},{5,7},{6,4},{7,5},{8,10},{9,11},{10,... | collective-permute-start | bytes 786440 | tf_op jit(solution)/shard_map/ppermute | solution.py:145
  16.5 4.6 %collective-permute-done.6 = bf16[32,4096]{1,0:T(8,128)(2,1)S(1)} collective-permute-done((bf16[32,4096]{1,0:T(8,128)(2,1)S(1)}, bf16[32,4096]{1,0:T(8,128)(2,1)S(1)}, u32[]{:S(2)}, u32[]{:S(2)}) %collective-permute-start.6) | collective-permute-done | bytes 262176 | tf_op jit(solution)/shard_map/ppermute | solution.py:145
  21.1 0.1 collective-permute-start.7
  21.2 0.0 copy-done.3
  21.2 0.0 copy-start
  21.2 3.1 %copy-done = bf16[256,14336]{1,0:T(8,128)(2,1)S(1)} copy-done((bf16[256,14336]{1,0:T(8,128)(2,1)S(1)}, bf16[256,14336]{1,0:T(8,128)(2,1)}, u32[]{:S(2)}) %copy-start) | copy-done | bytes 7340056
  24.3 0.0 copy-start.1
  24.3 1.6 %copy-done.1 = bf16[256,4096]{1,0:T(8,128)(2,1)S(1)} copy-done((bf16[256,4096]{1,0:T(8,128)(2,1)S(1)}, bf16[256,4096]{1,0:T(8,128)(2,1)}, u32[]{:S(2)}) %copy-start.1) | copy-done | bytes 2097176
  25.9 0.0 copy-start.2
  25.9 1.5 %copy-done.2 = bf16[64,14336]{1,0:T(8,128)(2,1)S(1)} copy-done((bf16[64,14336]{1,0:T(8,128)(2,1)S(1)}, bf16[64,14336]{1,0:T(8,128)(2,1)}, u32[]{:S(2)}) %copy-start.2) | copy-done | bytes 1835032
  27.4 7.0 %project.1 = (f32[64,128]{1,0:T(8,128)S(1)}, f32[64,128]{1,0:T(8,128)S(1)}) custom-call(bf16[256,4096]{1,0:T(8,128)(2,1)S(1)} %copy-done.1, bf16[256,14336]{1,0:T(8,128)(2,1)S(1)} %copy-done, bf16[64,4096]{1,0:T(8,128)(2,1)S(1)} %copy-done.3, bf16[64,14336]{1,0:T(8,128)(2,1)S(1)} %copy-done.2), custom_call_target="tpu_custom_call" | custom-call | flops 603979776 | bytes 11796480 | tf_op jit(solution)/shard_map/project/pallas_call | solution.py:53
  34.4 0.6 %collective-permute-start = (f32[64,128]{1,0:T(8,128)S(1)}, f32[64,128]{1,0:T(8,128)S(1)}, u32[]{:S(2)}, u32[]{:S(2)}) collective-permute-start(f32[64,128]{1,0:T(8,128)S(1)} %get-tuple-element.7), channel_id=1, source_target_pairs={{0,1},{1,0},{2,3},{3,2},{4,5},{5,4},{6,7},{7,6},{8,9},{9,8},{10,11... | collective-permute-start | bytes 98312 | tf_op jit(solution)/shard_map/ppermute | solution.py:145
  35.0 0.9 %collective-permute-done = f32[64,128]{1,0:T(8,128)S(1)} collective-permute-done((f32[64,128]{1,0:T(8,128)S(1)}, f32[64,128]{1,0:T(8,128)S(1)}, u32[]{:S(2)}, u32[]{:S(2)}) %collective-permute-start) | collective-permute-done | bytes 32800 | tf_op jit(solution)/shard_map/ppermute | solution.py:145
  35.8 3.2 %collective-permute-start.1 = (f32[64,128]{1,0:T(8,128)S(1)}, f32[64,128]{1,0:T(8,128)S(1)}, u32[]{:S(2)}, u32[]{:S(2)}) collective-permute-start(f32[64,128]{1,0:T(8,128)S(1)} %add.9), channel_id=1, source_target_pairs={{0,8},{1,9},{2,10},{3,11},{4,12},{5,13},{6,14},{7,15},{8,0},{9,1},... | collective-permute-start | bytes 98312 | tf_op jit(solution)/shard_map/ppermute | solution.py:145
  39.1 1.9 %collective-permute-done.1 = f32[64,128]{1,0:T(8,128)S(1)} collective-permute-done((f32[64,128]{1,0:T(8,128)S(1)}, f32[64,128]{1,0:T(8,128)S(1)}, u32[]{:S(2)}, u32[]{:S(2)}) %collective-permute-start.1) | collective-permute-done | bytes 32800 | tf_op jit(solution)/shard_map/ppermute | solution.py:145
  41.0 1.4 %collective-permute-start.2 = (f32[64,128]{1,0:T(8,128)S(1)}, f32[64,128]{1,0:T(8,128)S(1)}, u32[]{:S(2)}, u32[]{:S(2)}) collective-permute-start(f32[64,128]{1,0:T(8,128)S(1)} %add.10), channel_id=1, source_target_pairs={{0,4},{1,5},{2,6},{3,7},{4,0},{5,1},{6,2},{7,3},{8,12},{9,13},{10,... | collective-permute-start | bytes 98312 | tf_op jit(solution)/shard_map/ppermute | solution.py:145
  42.4 2.5 %collective-permute-done.2 = f32[64,128]{1,0:T(8,128)S(1)} collective-permute-done((f32[64,128]{1,0:T(8,128)S(1)}, f32[64,128]{1,0:T(8,128)S(1)}, u32[]{:S(2)}, u32[]{:S(2)}) %collective-permute-start.2) | collective-permute-done | bytes 32800 | tf_op jit(solution)/shard_map/ppermute | solution.py:145
  44.9 1.5 %collective-permute-start.3 = (f32[64,128]{1,0:T(8,128)S(1)}, f32[64,128]{1,0:T(8,128)S(1)}, u32[]{:S(2)}, u32[]{:S(2)}) collective-permute-start(f32[64,128]{1,0:T(8,128)S(1)} %add.11.m_ref), channel_id=1, source_target_pairs={{0,2},{1,3},{2,0},{3,1},{4,6},{5,7},{6,4},{7,5},{8,10},{9,11},{10,... | collective-permute-start | bytes 98312 | tf_op jit(solution)/shard_map/ppermute | solution.py:145
  46.4 2.4 %collective-permute-done.3.mr_ref = f32[64,128]{1,0:T(8,128)S(1)} collective-permute-done((f32[64,128]{1,0:T(8,128)S(1)}, f32[64,128]{1,0:T(8,128)S(1)}, u32[]{:S(2)}, u32[]{:S(2)}) %collective-permute-start.3) | collective-permute-done | bytes 32800 | tf_op jit(solution)/shard_map/ppermute | solution.py:145
  48.8 0.0 collective-permute-done.7.qb_ref
  48.8 4.1 %score.1 = f32[1,128]{1,0:T(1,128)} custom-call(f32[64,128]{1,0:T(8,128)S(1)} %add.11.m_ref, f32[64,128]{1,0:T(8,128)S(1)} %collective-permute-done.3.mr_ref, f32[64,128]{1,0:T(8,128)S(1)} %get-tuple-element.8.e_ref, bf16[64,4096]{1,0:T(8,128)(2,1)S(1)} %constant_dynamic-update-slice_fusion.qa_ref, bf16[64,4096]{1,0:T(8,128)(2,1)S(1)} %collective-permute-done.7.qb_ref), custom_call_target="tpu_custom_call" | custom-call | tf_op jit(solution)/shard_map/score/pallas_call | solution.py:159
  (6 shorter events, 0.0 us)
Async XLA Ops:
  0.0 21.2 %copy-start.3 = (bf16[64,4096]{1,0:T(8,128)(2,1)S(1)}, bf16[64,4096]{1,0:T(8,128)(2,1)}, u32[]{:S(2)}) copy-start(bf16[64,4096]{1,0:T(8,128)(2,1)} %pin_hbm.1) | copy-start | bytes 1572868
  0.0 7.9 %collective-permute-start.4 = (bf16[8,4096]{1,0:T(8,128)(2,1)}, bf16[8,4096]{1,0:T(8,128)(2,1)S(1)}, u32[]{:S(2)}, u32[]{:S(2)}) collective-permute-start(bf16[8,4096]{1,0:T(8,128)(2,1)} %param.9), channel_id=1, source_target_pairs={{0,8},{1,9},{2,10},{3,11},{4,12},{5,13},{6,14},{7,15},{8,0},{9,1},... | collective-permute-start | bytes 196616 | tf_op jit(solution)/shard_map/ppermute | solution.py:145
  8.7 5.0 %collective-permute-start.5 = (bf16[16,4096]{1,0:T(8,128)(2,1)S(1)}, bf16[16,4096]{1,0:T(8,128)(2,1)S(1)}, u32[]{:S(2)}, u32[]{:S(2)}) collective-permute-start(bf16[16,4096]{1,0:T(8,128)(2,1)S(1)} %pad_maximum_fusion.1), channel_id=1, source_target_pairs={{0,4},{1,5},{2,6},{3,7},{4,0},{5,1},{6,2},{7,3},{8,12},{9,13},{10,... | collective-permute-start | bytes 393224 | tf_op jit(solution)/shard_map/ppermute | solution.py:145
  14.6 6.4 %collective-permute-start.6 = (bf16[32,4096]{1,0:T(8,128)(2,1)S(1)}, bf16[32,4096]{1,0:T(8,128)(2,1)S(1)}, u32[]{:S(2)}, u32[]{:S(2)}) collective-permute-start(bf16[32,4096]{1,0:T(8,128)(2,1)S(1)} %pad_maximum_fusion), channel_id=1, source_target_pairs={{0,2},{1,3},{2,0},{3,1},{4,6},{5,7},{6,4},{7,5},{8,10},{9,11},{10,... | collective-permute-start | bytes 786440 | tf_op jit(solution)/shard_map/ppermute | solution.py:145
  21.1 27.7 %collective-permute-start.7 = (bf16[64,4096]{1,0:T(8,128)(2,1)S(1)}, bf16[64,4096]{1,0:T(8,128)(2,1)S(1)}, u32[]{:S(2)}, u32[]{:S(2)}) collective-permute-start(bf16[64,4096]{1,0:T(8,128)(2,1)S(1)} %constant_dynamic-update-slice_fusion.qa_ref), channel_id=1, source_target_pairs={{0,1},{1,0},{2,3},{3,2},{4,5},{5,4},{6,7},{7,6},{8,9},{9,8},{10,11... | collective-permute-start | bytes 1572872 | tf_op jit(solution)/shard_map/ppermute | solution.py:145
  21.2 3.1 %copy-start = (bf16[256,14336]{1,0:T(8,128)(2,1)S(1)}, bf16[256,14336]{1,0:T(8,128)(2,1)}, u32[]{:S(2)}) copy-start(bf16[256,14336]{1,0:T(8,128)(2,1)} %g_hbm.1) | copy-start | bytes 22020100
  24.3 1.6 %copy-start.1 = (bf16[256,4096]{1,0:T(8,128)(2,1)S(1)}, bf16[256,4096]{1,0:T(8,128)(2,1)}, u32[]{:S(2)}) copy-start(bf16[256,4096]{1,0:T(8,128)(2,1)} %x_hbm.1) | copy-start | bytes 6291460
  25.9 1.5 %copy-start.2 = (bf16[64,14336]{1,0:T(8,128)(2,1)S(1)}, bf16[64,14336]{1,0:T(8,128)(2,1)}, u32[]{:S(2)}) copy-start(bf16[64,14336]{1,0:T(8,128)(2,1)} %pout_hbm.1) | copy-start | bytes 5505028
  34.4 1.4 %collective-permute-start = (f32[64,128]{1,0:T(8,128)S(1)}, f32[64,128]{1,0:T(8,128)S(1)}, u32[]{:S(2)}, u32[]{:S(2)}) collective-permute-start(f32[64,128]{1,0:T(8,128)S(1)} %get-tuple-element.7), channel_id=1, source_target_pairs={{0,1},{1,0},{2,3},{3,2},{4,5},{5,4},{6,7},{7,6},{8,9},{9,8},{10,11... | collective-permute-start | bytes 98312 | tf_op jit(solution)/shard_map/ppermute | solution.py:145
  35.8 5.1 %collective-permute-start.1 = (f32[64,128]{1,0:T(8,128)S(1)}, f32[64,128]{1,0:T(8,128)S(1)}, u32[]{:S(2)}, u32[]{:S(2)}) collective-permute-start(f32[64,128]{1,0:T(8,128)S(1)} %add.9), channel_id=1, source_target_pairs={{0,8},{1,9},{2,10},{3,11},{4,12},{5,13},{6,14},{7,15},{8,0},{9,1},... | collective-permute-start | bytes 98312 | tf_op jit(solution)/shard_map/ppermute | solution.py:145
  41.0 3.9 %collective-permute-start.2 = (f32[64,128]{1,0:T(8,128)S(1)}, f32[64,128]{1,0:T(8,128)S(1)}, u32[]{:S(2)}, u32[]{:S(2)}) collective-permute-start(f32[64,128]{1,0:T(8,128)S(1)} %add.10), channel_id=1, source_target_pairs={{0,4},{1,5},{2,6},{3,7},{4,0},{5,1},{6,2},{7,3},{8,12},{9,13},{10,... | collective-permute-start | bytes 98312 | tf_op jit(solution)/shard_map/ppermute | solution.py:145
  44.9 3.9 %collective-permute-start.3 = (f32[64,128]{1,0:T(8,128)S(1)}, f32[64,128]{1,0:T(8,128)S(1)}, u32[]{:S(2)}, u32[]{:S(2)}) collective-permute-start(f32[64,128]{1,0:T(8,128)S(1)} %add.11.m_ref), channel_id=1, source_target_pairs={{0,2},{1,3},{2,0},{3,1},{4,6},{5,7},{6,4},{7,5},{8,10},{9,11},{10,... | collective-permute-start | bytes 98312 | tf_op jit(solution)/shard_map/ppermute | solution.py:145

commit v2 on v1

v2 whole, which is shorter than its diff:
```python
import functools
import math

import jax
import jax.numpy as jnp
from jax import lax
from jax.experimental import pallas as pl
from jax.experimental.pallas import tpu as pltpu
from jax.sharding import PartitionSpec as P

SEQ = 256
DAMPING = 0.1
CHUNK = 2048
PROJECT_MIB = 53.6
MIB = 1024 * 1024
HIGHEST = lax.Precision.HIGHEST


def project_kernel(rank, chunk, x_hbm, g_hbm, pin_hbm, pout_hbm, m_ref, e_ref, xt, gt, wi, wo, sems):
    x_count, g_count = xt.shape[0], gt.shape[0]

    def copies(src, dst, w_src, w_dst, base, k):
        part = pl.ds(pl.multiple_of(k * chunk, chunk), chunk)
        return (
            pltpu.make_async_copy(w_src.at[:, part], w_dst.at[k], sems.at[0, base + k]),
            pltpu.make_async_copy(src.at[:, part], dst.at[k], sems.at[1, base + k]),
        )

    x_copies = functools.partial(copies, x_hbm, xt, pin_hbm, wi, 0)
    g_copies = functools.partial(copies, g_hbm, gt, pout_hbm, wo, x_count)

    def start(make, k, carry):
        for copy in make(k):
            copy.start()
        return carry

    lax.fori_loop(0, x_count, functools.partial(start, x_copies), 0)
    lax.fori_loop(0, g_count, functools.partial(start, g_copies), 0)

    def multiply(make, tokens, weights, k, total):
        for copy in make(k):
            copy.wait()
        return total + lax.dot_general(
            weights[k], tokens[k], (((1,), (1,)), ((), ())), preferred_element_type=jnp.float32
        )

    zero = jnp.zeros((rank, xt.shape[1]), jnp.float32)
    x_low = lax.fori_loop(0, x_count, functools.partial(multiply, x_copies, xt, wi), zero)
    g_low = lax.fori_loop(0, g_count, functools.partial(multiply, g_copies, gt, wo), zero)
    a0, a1, a2 = split(jnp.concatenate([x_low, g_low], axis=0), 3)
    gram = lax.dot_general(
        jnp.concatenate([a0, a0, a1, a1, a0, a2], axis=1),
        jnp.concatenate([a0, a1, a0, a1, a2, a0], axis=1),
        (((1,), (1,)), ((), ())),
        preferred_element_type=jnp.float32,
    )
    lane = lax.broadcasted_iota(jnp.int32, (rank, 2 * rank), 1)
    m_ref[...] = jnp.where(lane < rank, gram[:rank], gram[rank:])
    e_ref[...] = gram[rank:]


def project(x, g, proj_in, proj_out):
    rank, rows = proj_in.shape[0], x.shape[0]
    chunk = math.gcd(math.gcd(x.shape[1], g.shape[1]), CHUNK)
    x_count, g_count = x.shape[1] // chunk, g.shape[1] // chunk
    out = jax.ShapeDtypeStruct((rank, 2 * rank), jnp.float32)
    return pl.pallas_call(
        functools.partial(project_kernel, rank, chunk),
        out_shape=(out, out),
        in_specs=[pl.BlockSpec(memory_space=pltpu.HBM)] * 4,
        out_specs=(pl.BlockSpec(memory_space=pltpu.VMEM),) * 2,
        scratch_shapes=[
            pltpu.VMEM((x_count, rows, chunk), x.dtype),
            pltpu.VMEM((g_count, rows, chunk), x.dtype),
            pltpu.VMEM((x_count, rank, chunk), x.dtype),
            pltpu.VMEM((g_count, rank, chunk), x.dtype),
            pltpu.SemaphoreType.DMA((2, x_count + g_count)),
        ],
        compiler_params=pltpu.CompilerParams(vmem_limit_bytes=int(PROJECT_MIB * MIB)),
        cost_estimate=pl.CostEstimate(
            flops=2 * rows * rank * (x.shape[1] + g.shape[1]),
            bytes_accessed=2 * (rows + rank) * (x.shape[1] + g.shape[1]),
            transcendentals=0,
        ),
        name="project",
    )(x, g, proj_in, proj_out)


def newton_scales(rank):
    low = 2.0 / (2.0 + rank / DAMPING)
    scales = []
    while 1.0 - low > 0.02:
        image = low * (2.0 - low)
        scale = 2.0 / (1.0 + image)
        scales.append(scale)
        low = scale * image
    return scales


def split(a, terms):
    parts = []
    for _ in range(terms):
        part = a.astype(jnp.bfloat16)
        parts.append(part)
        a = a - part.astype(jnp.float32)
    return parts


def dot(a, b):
    (a0, a1, a2), (b0, b1, b2) = split(a, 3), split(b, 3)
    left = jnp.concatenate([a0, a0, a1, a1, a0, a2], axis=1)
    right = jnp.concatenate([b0, b1, b0, b1, b2, b0], axis=0)
    return jnp.dot(left, right, preferred_element_type=jnp.float32)


def coarse_dot(a, b):
    (a0, a1), (b0, b1) = split(a, 2), split(b, 2)
    left = jnp.concatenate([a0, a1, a0], axis=1)
    right = jnp.concatenate([b0, b0, b1], axis=0)
    return jnp.dot(left, right, preferred_element_type=jnp.float32)


def invert_kernel(rank, tokens, m_ref, mr_ref, e_ref, flat_ref, rows_scr):
    size = 2 * rank
    total = (m_ref[...] + mr_ref[...]) * (1.0 / tokens)
    row = lax.broadcasted_iota(jnp.int32, (size, size), 0)
    col = lax.broadcasted_iota(jnp.int32, (size, size), 1)
    same = (row < rank) == (col < rank)
    eye = jnp.where(row == col, 1.0, 0.0)
    moment = jnp.where(same, jnp.concatenate([total, total], axis=0), 0.0)
    diagonal = jnp.where(row == col, moment, 0.0)
    by_col = jnp.sum(diagonal, axis=0, keepdims=True)
    half = lax.broadcasted_iota(jnp.int32, (1, size), 1) < rank
    trace_in = jnp.sum(jnp.where(half, by_col, 0.0), axis=1, keepdims=True)
    trace_out = jnp.sum(jnp.where(half, 0.0, by_col), axis=1, keepdims=True)
    damp = jnp.where(half, trace_in, trace_out) * (DAMPING / rank)
    a = moment + eye * damp
    first = (2.0 / (2.0 + rank / DAMPING)) / damp
    t = a * first
    for step, scale in enumerate(newton_scales(rank)):
        turn = scale * (2.0 * eye - t)
        if step == 0:
            x, t = turn * first, coarse_dot(t, turn)
        else:
            both = coarse_dot(jnp.concatenate([x, t], axis=0), turn)
            x, t = both[:size], both[size:]
    x = x + coarse_dot(x, eye - t)
    for _ in range(2):
        x = x + coarse_dot(x, eye - dot(a, x))
    pre = dot(dot(x[rank:, rank:], e_ref[:, :rank]), x[:rank, :])
    rows_scr[...] = pre
    even = rows_scr[pl.ds(0, rank // 2, stride=2), :]
    odd = rows_scr[pl.ds(1, rank // 2, stride=2), :]
    lane = lax.broadcasted_iota(jnp.int32, (rank // 2, size), 1)
    flat_ref[...] = jnp.where(lane < rank, even, pltpu.roll(odd, rank, 1))


def score_kernel(rank, slots, flat_ref, qa_ref, qb_ref, o_ref, acc_scr):
    size = 2 * rank
    me = lax.axis_index("dp")
    count = qa_ref.shape[0] // 16
    each = qa_ref.shape[0] * 2 // len(slots)
    for part, q_ref in enumerate((qa_ref, qb_ref)):
        for i in range(count):
            acc = jnp.zeros((16, size), jnp.float32)
            for j in range(rank // 2):
                block = q_ref[pl.ds(16 * i, 16), pl.ds(j * size, size)].astype(jnp.float32)
                acc = acc + block * flat_ref[j:j + 1, :]
            for h in range(2):
                slot = slots[part * 2 * count + 2 * i + h]
                acc_scr[pl.ds(pl.multiple_of((me ^ slot) * each, each), each), :] = acc[8 * h:8 * h + 8]
    ones = jnp.ones((8, size), jnp.float32)
    sums = lax.dot_general(
        ones, acc_scr[...], (((1,), (1,)), ((), ())), precision=HIGHEST, preferred_element_type=jnp.float32
    )
    o_ref[...] = sums[0:1] * (1.0 / rank)


def body(n, train_inputs, train_grads, proj_in, proj_out, query_grads):
    rank = proj_in.shape[0]
    steps = [1 << b for b in range(n.bit_length() - 1)]

    def swap(value, step):
        return lax.ppermute(value, "dp", [(i, i ^ step) for i in range(n)])

    moment, example = project(train_inputs, train_grads, proj_in, proj_out)
    far, near = steps[-1], steps[-2]
    slots = [0, far, near, far ^ near]
    pieces = [query_grads] + [swap(query_grads, step) for step in slots[1:]]
    moment, pieces = lax.optimization_barrier((moment, pieces))
    queries = jnp.concatenate(pieces[:2], axis=0)
    received = jnp.concatenate(pieces[2:], axis=0)
    for step in steps[-3::-1]:
        queries = jnp.concatenate([queries, received], axis=0)
        received = swap(queries, step)
        slots = slots + [slot ^ step for slot in slots]
    order = steps[:2] + steps[:1:-1]
    for step in order[:-1]:
        moment = moment + swap(moment, step)
    moment_far = swap(moment, order[-1])
    flat = pl.pallas_call(
        functools.partial(invert_kernel, rank, train_inputs.shape[0] * n),
        out_shape=jax.ShapeDtypeStruct((rank // 2, 2 * rank), jnp.float32),
        in_specs=[pl.BlockSpec(memory_space=pltpu.VMEM)] * 3,
        out_specs=pl.BlockSpec(memory_space=pltpu.VMEM),
        scratch_shapes=[pltpu.VMEM((rank, 2 * rank), jnp.float32)],
        compiler_params=pltpu.CompilerParams(vmem_limit_bytes=8 * MIB),
        cost_estimate=pl.CostEstimate(flops=10 ** 11, bytes_accessed=10 ** 5, transcendentals=0),
        name="invert",
    )(moment, moment_far, example)
    count = query_grads.shape[0] * n
    return pl.pallas_call(
        functools.partial(score_kernel, rank, slots),
        out_shape=jax.ShapeDtypeStruct((1, count), jnp.float32),
        in_specs=[pl.BlockSpec(memory_space=pltpu.VMEM)] * 3,
        out_specs=pl.BlockSpec(memory_space=pltpu.VMEM),
        scratch_shapes=[pltpu.VMEM((count, 2 * rank), jnp.float32)],
        compiler_params=pltpu.CompilerParams(vmem_limit_bytes=24 * MIB),
        name="score",
    )(flat, queries, received)


def solution(mesh):
    n = mesh.shape["dp"]
    return jax.shard_map(
        functools.partial(body, n),
        mesh=mesh,
        in_specs=(
            P(("groups", "dp"), None),
            P(("groups", "dp"), None),
            P(),
            P(),
            P(("groups", "dp"), None),
        ),
        out_specs=P(("groups", "dp"), None),
        check_vma=False,
    )
```

time: 53.3 us -> 29.5 us (0.55)
  waiting for transfers between devices: 19.6 us -> 9.49 us
  local copies, waits for them, and re-layouts: 7.08 us -> 0.04 us
  starting transfers between devices: 13.4 us -> 10.3 us
  Pallas kernels: 11.1 us -> 9.38 us
  other arithmetic: 1.72 us -> 0.04 us
    ppermute x8 -> x9, waiting for transfers between devices: 19.6 us -> 9.49 us  [swap(): return lax.ppermute(value, 'dp', [(i, i ^ step) for i in range(n)])]
    unnamed x11 -> x6, local copies, waits for them, and re-layouts: 7.06 us -> 0.03 us
    ppermute x8 -> x9, starting transfers between devices: 13.4 us -> 10.3 us  [swap(): return lax.ppermute(value, 'dp', [(i, i ^ step) for i in range(n)])]
    pallas_call x2 -> x3, Pallas kernels: 11.1 us -> 9.38 us  [the longest x1 5.79 us: project(): pl.pallas_call(functools.partial(project_kernel, rank, chunk), out_shape=...]
    concatenate x2 -> x1, other arithmetic: 1.71 us -> 0.02 us  [body(): queries = jnp.concatenate([queries, received], axis=0)]
  transfers between devices with their start and end apart: 8 -> 9, of which waited for: 7 -> 5; matrix products, arithmetic and copies ran while one was open for 2% -> 0% of each run, Pallas kernels for 13% -> 29%
where the time goes in v2:
time: 29.5 us; the launch traced here: 29.4 us
  starting transfers between devices  10.3 us (35%)
  waiting for transfers between devices  9.49 us (32%)
  Pallas kernels  9.38 us (32%)
    ppermute x9, starting transfers between devices, swap(): return lax.ppermute(value, 'dp', [(i, i ^ step) for i in range(n)])  10.3 us
    ppermute x9, waiting for transfers between devices, swap(): return lax.ppermute(value, 'dp', [(i, i ^ step) for i in range(n)])  9.49 us
    pallas_call x1, Pallas kernels, project(): pl.pallas_call(functools.partial(project_kernel, rank, chunk), out_shape=...  5.79 us
    pallas_call x1, Pallas kernels, body(): pl.pallas_call(functools.partial(invert_kernel, rank, train_inputs.shape[...  2.64 us
    pallas_call x1, Pallas kernels, body(): pl.pallas_call(functools.partial(score_kernel, rank, slots), out_shape=ja...  0.95 us
  transfers between devices with their start and end apart: 9, of which 5 were waited for; matrix products, arithmetic and copies ran while one was open for 0% of the time, Pallas kernels for 29%

profile of v2, /device:TPU:0, one launch (start us, length us, event | category | flops | bytes accessed | tf_op | source)
XLA Modules:
  0.0 29.4 jit_solution(11043419716028911434)
XLA Ops:
  0.0 0.0 copy-start
  0.0 4.0 %collective-permute-start = (bf16[8,4096]{1,0:T(8,128)(2,1)}, bf16[8,4096]{1,0:T(8,128)(2,1)S(1)}, u32[]{:S(2)}, u32[]{:S(2)}) collective-permute-start(bf16[8,4096]{1,0:T(8,128)(2,1)} %param.9), channel_id=1, source_target_pairs={{0,8},{1,9},{2,10},{3,11},{4,12},{5,13},{6,14},{7,15},{8,0},{9,1},... | collective-permute-start | bytes 196616 | tf_op jit(solution)/shard_map/ppermute | solution.py:184
  4.0 1.6 %collective-permute-start.1 = (bf16[8,4096]{1,0:T(8,128)(2,1)}, bf16[8,4096]{1,0:T(8,128)(2,1)S(1)}, u32[]{:S(2)}, u32[]{:S(2)}) collective-permute-start(bf16[8,4096]{1,0:T(8,128)(2,1)} %param.9), channel_id=1, source_target_pairs={{0,4},{1,5},{2,6},{3,7},{4,0},{5,1},{6,2},{7,3},{8,12},{9,13},{10,... | collective-permute-start | bytes 196616 | tf_op jit(solution)/shard_map/ppermute | solution.py:184
  5.6 0.0 collective-permute-start.2
  5.6 5.8 %project.1 = (f32[64,128]{1,0:T(8,128)S(1)}, f32[64,128]{1,0:T(8,128)S(1)}) custom-call(bf16[256,4096]{1,0:T(8,128)(2,1)} %x_hbm.1, bf16[256,14336]{1,0:T(8,128)(2,1)} %g_hbm.1, bf16[64,4096]{1,0:T(8,128)(2,1)} %pin_hbm.1, bf16[64,14336]{1,0:T(8,128)(2,1)} %pout_hbm.1), custom_call_target="tpu_custom_call" | custom-call | flops 603979776 | bytes 11796480 | tf_op jit(solution)/shard_map/project/pallas_call | solution.py:67
  11.4 0.0 collective-permute-done
  11.4 0.0 collective-permute-done.1
  11.4 0.4 %collective-permute-done.2 = bf16[8,4096]{1,0:T(8,128)(2,1)S(1)} collective-permute-done((bf16[8,4096]{1,0:T(8,128)(2,1)}, bf16[8,4096]{1,0:T(8,128)(2,1)S(1)}, u32[]{:S(2)}, u32[]{:S(2)}) %collective-permute-start.2) | collective-permute-done | bytes 65568 | tf_op jit(solution)/shard_map/ppermute | solution.py:184
  11.9 0.0 collective-permute-start.3
  11.9 0.0 copy-done
  11.9 1.1 %collective-permute-done.3 = f32[64,128]{1,0:T(8,128)S(1)} collective-permute-done((f32[64,128]{1,0:T(8,128)S(1)}, f32[64,128]{1,0:T(8,128)S(1)}, u32[]{:S(2)}, u32[]{:S(2)}) %collective-permute-start.3) | collective-permute-done | bytes 32800 | tf_op jit(solution)/shard_map/ppermute | solution.py:184
  13.1 1.5 %collective-permute-start.4 = (f32[64,128]{1,0:T(8,128)S(1)}, f32[64,128]{1,0:T(8,128)S(1)}, u32[]{:S(2)}, u32[]{:S(2)}) collective-permute-start(f32[64,128]{1,0:T(8,128)S(1)} %add.9), channel_id=1, source_target_pairs={{0,2},{1,3},{2,0},{3,1},{4,6},{5,7},{6,4},{7,5},{8,10},{9,11},{10,... | collective-permute-start | bytes 98312 | tf_op jit(solution)/shard_map/ppermute | solution.py:184
  14.6 0.5 %collective-permute-start.7 = (bf16[32,4096]{1,0:T(8,128)(2,1)S(1)}, bf16[32,4096]{1,0:T(8,128)(2,1)S(1)}, u32[]{:S(2)}, u32[]{:S(2)}) collective-permute-start(bf16[32,4096]{1,0:T(8,128)(2,1)S(1)} %pad_maximum_fusion), channel_id=1, source_target_pairs={{0,2},{1,3},{2,0},{3,1},{4,6},{5,7},{6,4},{7,5},{8,10},{9,11},{10,... | collective-permute-start | bytes 786440 | tf_op jit(solution)/shard_map/ppermute | solution.py:184
  15.1 1.9 %collective-permute-done.4 = f32[64,128]{1,0:T(8,128)S(1)} collective-permute-done((f32[64,128]{1,0:T(8,128)S(1)}, f32[64,128]{1,0:T(8,128)S(1)}, u32[]{:S(2)}, u32[]{:S(2)}) %collective-permute-start.4) | collective-permute-done | bytes 32800 | tf_op jit(solution)/shard_map/ppermute | solution.py:184
  17.0 1.5 %collective-permute-start.5 = (f32[64,128]{1,0:T(8,128)S(1)}, f32[64,128]{1,0:T(8,128)S(1)}, u32[]{:S(2)}, u32[]{:S(2)}) collective-permute-start(f32[64,128]{1,0:T(8,128)S(1)} %add.10), channel_id=1, source_target_pairs={{0,8},{1,9},{2,10},{3,11},{4,12},{5,13},{6,14},{7,15},{8,0},{9,1},... | collective-permute-start | bytes 98312 | tf_op jit(solution)/shard_map/ppermute | solution.py:184
  18.6 3.3 %collective-permute-done.5 = f32[64,128]{1,0:T(8,128)S(1)} collective-permute-done((f32[64,128]{1,0:T(8,128)S(1)}, f32[64,128]{1,0:T(8,128)S(1)}, u32[]{:S(2)}, u32[]{:S(2)}) %collective-permute-start.5) | collective-permute-done | bytes 32800 | tf_op jit(solution)/shard_map/ppermute | solution.py:184
  21.8 1.1 %collective-permute-start.6 = (f32[64,128]{1,0:T(8,128)S(1)}, f32[64,128]{1,0:T(8,128)S(1)}, u32[]{:S(2)}, u32[]{:S(2)}) collective-permute-start(f32[64,128]{1,0:T(8,128)S(1)} %add.11.m_ref), channel_id=1, source_target_pairs={{0,4},{1,5},{2,6},{3,7},{4,0},{5,1},{6,2},{7,3},{8,12},{9,13},{10,... | collective-permute-start | bytes 98312 | tf_op jit(solution)/shard_map/ppermute | solution.py:184
  22.9 0.0 collective-permute-done.7
  23.0 0.1 collective-permute-start.8
  23.0 2.7 %collective-permute-done.6.mr_ref = f32[64,128]{1,0:T(8,128)S(1)} collective-permute-done((f32[64,128]{1,0:T(8,128)S(1)}, f32[64,128]{1,0:T(8,128)S(1)}, u32[]{:S(2)}, u32[]{:S(2)}) %collective-permute-start.6) | collective-permute-done | bytes 32800 | tf_op jit(solution)/shard_map/ppermute | solution.py:184
  25.8 2.6 %invert.1.flat_ref = f32[32,128]{1,0:T(8,128)S(1)} custom-call(f32[64,128]{1,0:T(8,128)S(1)} %add.11.m_ref, f32[64,128]{1,0:T(8,128)S(1)} %collective-permute-done.6.mr_ref, f32[64,128]{1,0:T(8,128)S(1)} %get-tuple-element.14.e_ref), custom_call_target="tpu_custom_call" | custom-call | flops 99999997952 | bytes 100000 | tf_op jit(solution)/shard_map/invert/pallas_call | solution.py:201
  28.4 0.0 collective-permute-done.8.qb_ref
  28.4 0.9 %score.1 = f32[1,128]{1,0:T(1,128)} custom-call(f32[32,128]{1,0:T(8,128)S(1)} %invert.1.flat_ref, bf16[64,4096]{1,0:T(8,128)(2,1)S(1)} %constant_dynamic-update-slice_fusion.qa_ref, bf16[64,4096]{1,0:T(8,128)(2,1)S(1)} %collective-permute-done.8.qb_ref), custom_call_target="tpu_custom_call" | custom-call | tf_op jit(solution)/shard_map/score/pallas_call | solution.py:212
  (9 shorter events, 0.1 us)
Async XLA Ops:
  0.0 11.9 %copy-start = (bf16[8,4096]{1,0:T(8,128)(2,1)S(1)}, bf16[8,4096]{1,0:T(8,128)(2,1)}, u32[]{:S(2)}) copy-start(bf16[8,4096]{1,0:T(8,128)(2,1)} %param.9) | copy-start | bytes 196612
  0.0 11.4 %collective-permute-start = (bf16[8,4096]{1,0:T(8,128)(2,1)}, bf16[8,4096]{1,0:T(8,128)(2,1)S(1)}, u32[]{:S(2)}, u32[]{:S(2)}) collective-permute-start(bf16[8,4096]{1,0:T(8,128)(2,1)} %param.9), channel_id=1, source_target_pairs={{0,8},{1,9},{2,10},{3,11},{4,12},{5,13},{6,14},{7,15},{8,0},{9,1},... | collective-permute-start | bytes 196616 | tf_op jit(solution)/shard_map/ppermute | solution.py:184
  4.0 7.4 %collective-permute-start.1 = (bf16[8,4096]{1,0:T(8,128)(2,1)}, bf16[8,4096]{1,0:T(8,128)(2,1)S(1)}, u32[]{:S(2)}, u32[]{:S(2)}) collective-permute-start(bf16[8,4096]{1,0:T(8,128)(2,1)} %param.9), channel_id=1, source_target_pairs={{0,4},{1,5},{2,6},{3,7},{4,0},{5,1},{6,2},{7,3},{8,12},{9,13},{10,... | collective-permute-start | bytes 196616 | tf_op jit(solution)/shard_map/ppermute | solution.py:184
  5.6 6.3 %collective-permute-start.2 = (bf16[8,4096]{1,0:T(8,128)(2,1)}, bf16[8,4096]{1,0:T(8,128)(2,1)S(1)}, u32[]{:S(2)}, u32[]{:S(2)}) collective-permute-start(bf16[8,4096]{1,0:T(8,128)(2,1)} %param.9), channel_id=1, source_target_pairs={{0,12},{1,13},{2,14},{3,15},{4,8},{5,9},{6,10},{7,11},{8,4},{9,5},... | collective-permute-start | bytes 196616 | tf_op jit(solution)/shard_map/ppermute | solution.py:184
  11.9 1.2 %collective-permute-start.3 = (f32[64,128]{1,0:T(8,128)S(1)}, f32[64,128]{1,0:T(8,128)S(1)}, u32[]{:S(2)}, u32[]{:S(2)}) collective-permute-start(f32[64,128]{1,0:T(8,128)S(1)} %get-tuple-element.13), channel_id=1, source_target_pairs={{0,1},{1,0},{2,3},{3,2},{4,5},{5,4},{6,7},{7,6},{8,9},{9,8},{10,11... | collective-permute-start | bytes 98312 | tf_op jit(solution)/shard_map/ppermute | solution.py:184
  13.1 3.9 %collective-permute-start.4 = (f32[64,128]{1,0:T(8,128)S(1)}, f32[64,128]{1,0:T(8,128)S(1)}, u32[]{:S(2)}, u32[]{:S(2)}) collective-permute-start(f32[64,128]{1,0:T(8,128)S(1)} %add.9), channel_id=1, source_target_pairs={{0,2},{1,3},{2,0},{3,1},{4,6},{5,7},{6,4},{7,5},{8,10},{9,11},{10,... | collective-permute-start | bytes 98312 | tf_op jit(solution)/shard_map/ppermute | solution.py:184
  14.6 8.3 %collective-permute-start.7 = (bf16[32,4096]{1,0:T(8,128)(2,1)S(1)}, bf16[32,4096]{1,0:T(8,128)(2,1)S(1)}, u32[]{:S(2)}, u32[]{:S(2)}) collective-permute-start(bf16[32,4096]{1,0:T(8,128)(2,1)S(1)} %pad_maximum_fusion), channel_id=1, source_target_pairs={{0,2},{1,3},{2,0},{3,1},{4,6},{5,7},{6,4},{7,5},{8,10},{9,11},{10,... | collective-permute-start | bytes 786440 | tf_op jit(solution)/shard_map/ppermute | solution.py:184
  17.0 4.8 %collective-permute-start.5 = (f32[64,128]{1,0:T(8,128)S(1)}, f32[64,128]{1,0:T(8,128)S(1)}, u32[]{:S(2)}, u32[]{:S(2)}) collective-permute-start(f32[64,128]{1,0:T(8,128)S(1)} %add.10), channel_id=1, source_target_pairs={{0,8},{1,9},{2,10},{3,11},{4,12},{5,13},{6,14},{7,15},{8,0},{9,1},... | collective-permute-start | bytes 98312 | tf_op jit(solution)/shard_map/ppermute | solution.py:184
  21.8 3.9 %collective-permute-start.6 = (f32[64,128]{1,0:T(8,128)S(1)}, f32[64,128]{1,0:T(8,128)S(1)}, u32[]{:S(2)}, u32[]{:S(2)}) collective-permute-start(f32[64,128]{1,0:T(8,128)S(1)} %add.11.m_ref), channel_id=1, source_target_pairs={{0,4},{1,5},{2,6},{3,7},{4,0},{5,1},{6,2},{7,3},{8,12},{9,13},{10,... | collective-permute-start | bytes 98312 | tf_op jit(solution)/shard_map/ppermute | solution.py:184
  23.0 5.4 %collective-permute-start.8 = (bf16[64,4096]{1,0:T(8,128)(2,1)S(1)}, bf16[64,4096]{1,0:T(8,128)(2,1)S(1)}, u32[]{:S(2)}, u32[]{:S(2)}) collective-permute-start(bf16[64,4096]{1,0:T(8,128)(2,1)S(1)} %constant_dynamic-update-slice_fusion.qa_ref), channel_id=1, source_target_pairs={{0,1},{1,0},{2,3},{3,2},{4,5},{5,4},{6,7},{7,6},{8,9},{9,8},{10,11... | collective-permute-start | bytes 1572872 | tf_op jit(solution)/shard_map/ppermute | solution.py:184

commit v3 on v2

--- a/solution.py
+++ b/solution.py
@@ -122,14 +122,18 @@
 
 def invert_kernel(rank, tokens, m_ref, mr_ref, e_ref, flat_ref, rows_scr):
     size = 2 * rank
-    total = (m_ref[...] + mr_ref[...]) * (1.0 / tokens)
-    row = lax.broadcasted_iota(jnp.int32, (size, size), 0)
-    col = lax.broadcasted_iota(jnp.int32, (size, size), 1)
-    same = (row < rank) == (col < rank)
-    eye = jnp.where(row == col, 1.0, 0.0)
-    moment = jnp.where(same, jnp.concatenate([total, total], axis=0), 0.0)
-    diagonal = jnp.where(row == col, moment, 0.0)
-    by_col = jnp.sum(diagonal, axis=0, keepdims=True)
+    low = lax.broadcasted_iota(jnp.int32, (rank, size), 1) < rank
+    row = lax.broadcasted_iota(jnp.int32, (rank, size), 0)
+    col = lax.broadcasted_iota(jnp.int32, (rank, size), 1)
+    on_diagonal = jnp.where(low, col, col - rank) == row
+    eye = jnp.where(on_diagonal, 1.0, 0.0)
+
+    def blocks(pair):
+        zero = jnp.zeros_like(pair)
+        return jnp.concatenate([jnp.where(low, pair, zero), jnp.where(low, zero, pair)], axis=0)
+
+    moment = (m_ref[...] + mr_ref[...]) * (1.0 / tokens)
+    by_col = jnp.sum(jnp.where(on_diagonal, moment, 0.0), axis=0, keepdims=True)
     half = lax.broadcasted_iota(jnp.int32, (1, size), 1) < rank
     trace_in = jnp.sum(jnp.where(half, by_col, 0.0), axis=1, keepdims=True)
     trace_out = jnp.sum(jnp.where(half, 0.0, by_col), axis=1, keepdims=True)
@@ -140,15 +144,17 @@
     for step, scale in enumerate(newton_scales(rank)):
         turn = scale * (2.0 * eye - t)
         if step == 0:
-            x, t = turn * first, coarse_dot(t, turn)
+            x, t = turn * first, coarse_dot(t, blocks(turn))
         else:
-            both = coarse_dot(jnp.concatenate([x, t], axis=0), turn)
-            x, t = both[:size], both[size:]
-    x = x + coarse_dot(x, eye - t)
+            both = coarse_dot(jnp.concatenate([x, t], axis=0), blocks(turn))
+            x, t = both[:rank], both[rank:]
+    x = x + coarse_dot(x, blocks(eye - t))
     for _ in range(2):
-        x = x + coarse_dot(x, eye - dot(a, x))
-    pre = dot(dot(x[rank:, rank:], e_ref[:, :rank]), x[:rank, :])
-    rows_scr[...] = pre
+        x = x + coarse_dot(x, blocks(eye - dot(a, blocks(x))))
+    inverses = blocks(x)
+    example = jnp.where(low, e_ref[...], 0.0)
+    left = dot(inverses[rank:], jnp.concatenate([jnp.zeros_like(example), example], axis=0))
+    rows_scr[...] = dot(left, jnp.concatenate([inverses[:rank], jnp.zeros_like(example)], axis=0))
     even = rows_scr[pl.ds(0, rank // 2, stride=2), :]
     odd = rows_scr[pl.ds(1, rank // 2, stride=2), :]
     lane = lax.broadcasted_iota(jnp.int32, (rank // 2, size), 1)
@@ -187,17 +193,22 @@
     far, near = steps[-1], steps[-2]
     slots = [0, far, near, far ^ near]
     pieces = [query_grads] + [swap(query_grads, step) for step in slots[1:]]
-    moment, pieces = lax.optimization_barrier((moment, pieces))
+    moment, early = lax.optimization_barrier((moment, pieces[:2]))
+    sums, order = [moment], steps[:2] + steps[:1:-1]
+    for step in order[:-1]:
+        sums.append(sums[-1] + swap(sums[-1], step))
+    moment, moment_far = sums[-1], swap(sums[-1], order[-1])
+
+    def beside(k, value):
+        return lax.optimization_barrier((sums[k], value))[1]
+
+    pieces = early + [beside(1, piece) for piece in pieces[2:]]
     queries = jnp.concatenate(pieces[:2], axis=0)
     received = jnp.concatenate(pieces[2:], axis=0)
     for step in steps[-3::-1]:
         queries = jnp.concatenate([queries, received], axis=0)
-        received = swap(queries, step)
+        received = swap(beside(1, queries) if step == steps[1] else queries, step)
         slots = slots + [slot ^ step for slot in slots]
-    order = steps[:2] + steps[:1:-1]
-    for step in order[:-1]:
-        moment = moment + swap(moment, step)
-    moment_far = swap(moment, order[-1])
     flat = pl.pallas_call(
         functools.partial(invert_kernel, rank, train_inputs.shape[0] * n),
         out_shape=jax.ShapeDtypeStruct((rank // 2, 2 * rank), jnp.float32),

time: 29.5 us -> 28.7 us (0.973)
  waiting for transfers between devices: 9.49 us -> 8.2 us
  starting transfers between devices: 10.3 us -> 11.2 us
  Pallas kernels: 9.38 us -> 9.01 us
    ppermute x9, waiting for transfers between devices: 9.49 us -> 8.2 us  [swap(): return lax.ppermute(value, 'dp', [(i, i ^ step) for i in range(n)])]
    ppermute x9, starting transfers between devices: 10.3 us -> 11.2 us  [swap(): return lax.ppermute(value, 'dp', [(i, i ^ step) for i in range(n)])]
    pallas_call x1, Pallas kernels: 2.64 us -> 2.27 us  [body(): pl.pallas_call(functools.partial(invert_kernel, rank, train_inputs.shape[...]
  transfers between devices with their start and end apart: 9 -> 9, of which waited for: 5 -> 4; matrix products, arithmetic and copies ran while one was open for 0% -> 0% of each run, Pallas kernels for 29% -> 28%
where the time goes in v3:
time: 28.7 us; the launch traced here: 28.6 us
  starting transfers between devices  11.2 us (39%)
  Pallas kernels  9.01 us (31%)
  waiting for transfers between devices  8.2 us (29%)
    ppermute x9, starting transfers between devices, swap(): return lax.ppermute(value, 'dp', [(i, i ^ step) for i in range(n)])  11.2 us
    ppermute x9, waiting for transfers between devices, swap(): return lax.ppermute(value, 'dp', [(i, i ^ step) for i in range(n)])  8.2 us
    pallas_call x1, Pallas kernels, project(): pl.pallas_call(functools.partial(project_kernel, rank, chunk), out_shape=...  5.79 us
    pallas_call x1, Pallas kernels, body(): pl.pallas_call(functools.partial(invert_kernel, rank, train_inputs.shape[...  2.27 us
    pallas_call x1, Pallas kernels, body(): pl.pallas_call(functools.partial(score_kernel, rank, slots), out_shape=ja...  0.95 us
  transfers between devices with their start and end apart: 9, of which 4 were waited for; matrix products, arithmetic and copies ran while one was open for 0% of the time, Pallas kernels for 28%

profile of v3, /device:TPU:0, one launch (start us, length us, event | category | flops | bytes accessed | tf_op | source)
XLA Modules:
  0.0 28.6 jit_solution(16960072692383987490)
XLA Ops:
  0.0 0.0 copy-start
  0.0 4.0 %collective-permute-start = (bf16[8,4096]{1,0:T(8,128)(2,1)}, bf16[8,4096]{1,0:T(8,128)(2,1)S(1)}, u32[]{:S(2)}, u32[]{:S(2)}) collective-permute-start(bf16[8,4096]{1,0:T(8,128)(2,1)} %param.9), channel_id=1, source_target_pairs={{0,8},{1,9},{2,10},{3,11},{4,12},{5,13},{6,14},{7,15},{8,0},{9,1},... | collective-permute-start | bytes 196616 | tf_op jit(solution)/shard_map/ppermute | solution.py:190
  4.0 1.6 %collective-permute-start.5 = (bf16[8,4096]{1,0:T(8,128)(2,1)}, bf16[8,4096]{1,0:T(8,128)(2,1)S(1)}, u32[]{:S(2)}, u32[]{:S(2)}) collective-permute-start(bf16[8,4096]{1,0:T(8,128)(2,1)} %param.9), channel_id=1, source_target_pairs={{0,4},{1,5},{2,6},{3,7},{4,0},{5,1},{6,2},{7,3},{8,12},{9,13},{10,... | collective-permute-start | bytes 196616 | tf_op jit(solution)/shard_map/ppermute | solution.py:190
  5.6 0.0 collective-permute-start.6
  5.6 5.8 %project.1 = (f32[64,128]{1,0:T(8,128)S(1)}, f32[64,128]{1,0:T(8,128)S(1)}) custom-call(bf16[256,4096]{1,0:T(8,128)(2,1)} %x_hbm.1, bf16[256,14336]{1,0:T(8,128)(2,1)} %g_hbm.1, bf16[64,4096]{1,0:T(8,128)(2,1)} %pin_hbm.1, bf16[64,14336]{1,0:T(8,128)(2,1)} %pout_hbm.1), custom_call_target="tpu_custom_call" | custom-call | flops 603979776 | bytes 11796480 | tf_op jit(solution)/shard_map/project/pallas_call | solution.py:67
  11.4 0.0 collective-permute-done
  11.4 0.1 collective-permute-start.1
  11.5 0.0 copy-done
  11.5 1.2 %collective-permute-done.1 = f32[64,128]{1,0:T(8,128)S(1)} collective-permute-done((f32[64,128]{1,0:T(8,128)S(1)}, f32[64,128]{1,0:T(8,128)S(1)}, u32[]{:S(2)}, u32[]{:S(2)}) %collective-permute-start.1) | collective-permute-done | bytes 32800 | tf_op jit(solution)/shard_map/ppermute | solution.py:190
  12.7 1.7 %collective-permute-start.2 = (f32[64,128]{1,0:T(8,128)S(1)}, f32[64,128]{1,0:T(8,128)S(1)}, u32[]{:S(2)}, u32[]{:S(2)}) collective-permute-start(f32[64,128]{1,0:T(8,128)S(1)} %add.9), channel_id=1, source_target_pairs={{0,2},{1,3},{2,0},{3,1},{4,6},{5,7},{6,4},{7,5},{8,10},{9,11},{10,... | collective-permute-start | bytes 98312 | tf_op jit(solution)/shard_map/ppermute | solution.py:190
  14.4 0.0 collective-permute-done.5
  14.4 0.0 collective-permute-done.6
  14.5 0.4 %collective-permute-start.7 = (bf16[32,4096]{1,0:T(8,128)(2,1)S(1)}, bf16[32,4096]{1,0:T(8,128)(2,1)S(1)}, u32[]{:S(2)}, u32[]{:S(2)}) collective-permute-start(bf16[32,4096]{1,0:T(8,128)(2,1)S(1)} %pad_maximum_fusion), channel_id=1, source_target_pairs={{0,2},{1,3},{2,0},{3,1},{4,6},{5,7},{6,4},{7,5},{8,10},{9,11},{10,... | collective-permute-start | bytes 786440 | tf_op jit(solution)/shard_map/ppermute | solution.py:190
  14.8 1.8 %collective-permute-done.2 = f32[64,128]{1,0:T(8,128)S(1)} collective-permute-done((f32[64,128]{1,0:T(8,128)S(1)}, f32[64,128]{1,0:T(8,128)S(1)}, u32[]{:S(2)}, u32[]{:S(2)}) %collective-permute-start.2) | collective-permute-done | bytes 32800 | tf_op jit(solution)/shard_map/ppermute | solution.py:190
  16.6 1.9 %collective-permute-start.3 = (f32[64,128]{1,0:T(8,128)S(1)}, f32[64,128]{1,0:T(8,128)S(1)}, u32[]{:S(2)}, u32[]{:S(2)}) collective-permute-start(f32[64,128]{1,0:T(8,128)S(1)} %add.10), channel_id=1, source_target_pairs={{0,8},{1,9},{2,10},{3,11},{4,12},{5,13},{6,14},{7,15},{8,0},{9,1},... | collective-permute-start | bytes 98312 | tf_op jit(solution)/shard_map/ppermute | solution.py:190
  18.5 2.9 %collective-permute-done.3 = f32[64,128]{1,0:T(8,128)S(1)} collective-permute-done((f32[64,128]{1,0:T(8,128)S(1)}, f32[64,128]{1,0:T(8,128)S(1)}, u32[]{:S(2)}, u32[]{:S(2)}) %collective-permute-start.3) | collective-permute-done | bytes 32800 | tf_op jit(solution)/shard_map/ppermute | solution.py:190
  21.5 1.5 %collective-permute-start.4 = (f32[64,128]{1,0:T(8,128)S(1)}, f32[64,128]{1,0:T(8,128)S(1)}, u32[]{:S(2)}, u32[]{:S(2)}) collective-permute-start(f32[64,128]{1,0:T(8,128)S(1)} %add.11.m_ref), channel_id=1, source_target_pairs={{0,4},{1,5},{2,6},{3,7},{4,0},{5,1},{6,2},{7,3},{8,12},{9,13},{10,... | collective-permute-start | bytes 98312 | tf_op jit(solution)/shard_map/ppermute | solution.py:190
  22.9 0.0 collective-permute-done.7
  22.9 0.1 collective-permute-start.8
  23.0 2.4 %collective-permute-done.4.mr_ref = f32[64,128]{1,0:T(8,128)S(1)} collective-permute-done((f32[64,128]{1,0:T(8,128)S(1)}, f32[64,128]{1,0:T(8,128)S(1)}, u32[]{:S(2)}, u32[]{:S(2)}) %collective-permute-start.4) | collective-permute-done | bytes 32800 | tf_op jit(solution)/shard_map/ppermute | solution.py:190
  25.4 2.3 %invert.1.flat_ref = f32[32,128]{1,0:T(8,128)S(1)} custom-call(f32[64,128]{1,0:T(8,128)S(1)} %add.11.m_ref, f32[64,128]{1,0:T(8,128)S(1)} %collective-permute-done.4.mr_ref, f32[64,128]{1,0:T(8,128)S(1)} %get-tuple-element.15.e_ref), custom_call_target="tpu_custom_call" | custom-call | flops 99999997952 | bytes 100000 | tf_op jit(solution)/shard_map/invert/pallas_call | solution.py:212
  27.6 0.0 collective-permute-done.8.qb_ref
  27.6 0.9 %score.1 = f32[1,128]{1,0:T(1,128)} custom-call(f32[32,128]{1,0:T(8,128)S(1)} %invert.1.flat_ref, bf16[64,4096]{1,0:T(8,128)(2,1)S(1)} %constant_dynamic-update-slice_fusion.qa_ref, bf16[64,4096]{1,0:T(8,128)(2,1)S(1)} %collective-permute-done.8.qb_ref), custom_call_target="tpu_custom_call" | custom-call | tf_op jit(solution)/shard_map/score/pallas_call | solution.py:223
  (9 shorter events, 0.1 us)
Async XLA Ops:
  0.0 11.5 %copy-start = (bf16[8,4096]{1,0:T(8,128)(2,1)S(1)}, bf16[8,4096]{1,0:T(8,128)(2,1)}, u32[]{:S(2)}) copy-start(bf16[8,4096]{1,0:T(8,128)(2,1)} %param.9) | copy-start | bytes 196612
  0.0 11.4 %collective-permute-start = (bf16[8,4096]{1,0:T(8,128)(2,1)}, bf16[8,4096]{1,0:T(8,128)(2,1)S(1)}, u32[]{:S(2)}, u32[]{:S(2)}) collective-permute-start(bf16[8,4096]{1,0:T(8,128)(2,1)} %param.9), channel_id=1, source_target_pairs={{0,8},{1,9},{2,10},{3,11},{4,12},{5,13},{6,14},{7,15},{8,0},{9,1},... | collective-permute-start | bytes 196616 | tf_op jit(solution)/shard_map/ppermute | solution.py:190
  4.0 10.4 %collective-permute-start.5 = (bf16[8,4096]{1,0:T(8,128)(2,1)}, bf16[8,4096]{1,0:T(8,128)(2,1)S(1)}, u32[]{:S(2)}, u32[]{:S(2)}) collective-permute-start(bf16[8,4096]{1,0:T(8,128)(2,1)} %param.9), channel_id=1, source_target_pairs={{0,4},{1,5},{2,6},{3,7},{4,0},{5,1},{6,2},{7,3},{8,12},{9,13},{10,... | collective-permute-start | bytes 196616 | tf_op jit(solution)/shard_map/ppermute | solution.py:190
  5.6 8.8 %collective-permute-start.6 = (bf16[8,4096]{1,0:T(8,128)(2,1)}, bf16[8,4096]{1,0:T(8,128)(2,1)S(1)}, u32[]{:S(2)}, u32[]{:S(2)}) collective-permute-start(bf16[8,4096]{1,0:T(8,128)(2,1)} %param.9), channel_id=1, source_target_pairs={{0,12},{1,13},{2,14},{3,15},{4,8},{5,9},{6,10},{7,11},{8,4},{9,5},... | collective-permute-start | bytes 196616 | tf_op jit(solution)/shard_map/ppermute | solution.py:190
  11.4 1.3 %collective-permute-start.1 = (f32[64,128]{1,0:T(8,128)S(1)}, f32[64,128]{1,0:T(8,128)S(1)}, u32[]{:S(2)}, u32[]{:S(2)}) collective-permute-start(f32[64,128]{1,0:T(8,128)S(1)} %get-tuple-element.14), channel_id=1, source_target_pairs={{0,1},{1,0},{2,3},{3,2},{4,5},{5,4},{6,7},{7,6},{8,9},{9,8},{10,11... | collective-permute-start | bytes 98312 | tf_op jit(solution)/shard_map/ppermute | solution.py:190
  12.7 3.9 %collective-permute-start.2 = (f32[64,128]{1,0:T(8,128)S(1)}, f32[64,128]{1,0:T(8,128)S(1)}, u32[]{:S(2)}, u32[]{:S(2)}) collective-permute-start(f32[64,128]{1,0:T(8,128)S(1)} %add.9), channel_id=1, source_target_pairs={{0,2},{1,3},{2,0},{3,1},{4,6},{5,7},{6,4},{7,5},{8,10},{9,11},{10,... | collective-permute-start | bytes 98312 | tf_op jit(solution)/shard_map/ppermute | solution.py:190
  14.5 8.4 %collective-permute-start.7 = (bf16[32,4096]{1,0:T(8,128)(2,1)S(1)}, bf16[32,4096]{1,0:T(8,128)(2,1)S(1)}, u32[]{:S(2)}, u32[]{:S(2)}) collective-permute-start(bf16[32,4096]{1,0:T(8,128)(2,1)S(1)} %pad_maximum_fusion), channel_id=1, source_target_pairs={{0,2},{1,3},{2,0},{3,1},{4,6},{5,7},{6,4},{7,5},{8,10},{9,11},{10,... | collective-permute-start | bytes 786440 | tf_op jit(solution)/shard_map/ppermute | solution.py:190
  16.6 4.8 %collective-permute-start.3 = (f32[64,128]{1,0:T(8,128)S(1)}, f32[64,128]{1,0:T(8,128)S(1)}, u32[]{:S(2)}, u32[]{:S(2)}) collective-permute-start(f32[64,128]{1,0:T(8,128)S(1)} %add.10), channel_id=1, source_target_pairs={{0,8},{1,9},{2,10},{3,11},{4,12},{5,13},{6,14},{7,15},{8,0},{9,1},... | collective-permute-start | bytes 98312 | tf_op jit(solution)/shard_map/ppermute | solution.py:190
  21.5 3.9 %collective-permute-start.4 = (f32[64,128]{1,0:T(8,128)S(1)}, f32[64,128]{1,0:T(8,128)S(1)}, u32[]{:S(2)}, u32[]{:S(2)}) collective-permute-start(f32[64,128]{1,0:T(8,128)S(1)} %add.11.m_ref), channel_id=1, source_target_pairs={{0,4},{1,5},{2,6},{3,7},{4,0},{5,1},{6,2},{7,3},{8,12},{9,13},{10,... | collective-permute-start | bytes 98312 | tf_op jit(solution)/shard_map/ppermute | solution.py:190
  22.9 4.7 %collective-permute-start.8 = (bf16[64,4096]{1,0:T(8,128)(2,1)S(1)}, bf16[64,4096]{1,0:T(8,128)(2,1)S(1)}, u32[]{:S(2)}, u32[]{:S(2)}) collective-permute-start(bf16[64,4096]{1,0:T(8,128)(2,1)S(1)} %constant_dynamic-update-slice_fusion.qa_ref), channel_id=1, source_target_pairs={{0,1},{1,0},{2,3},{3,2},{4,5},{5,4},{6,7},{7,6},{8,9},{9,8},{10,11... | collective-permute-start | bytes 1572872 | tf_op jit(solution)/shard_map/ppermute | solution.py:190

commit v4 on v3

--- a/solution.py
+++ b/solution.py
@@ -148,7 +148,6 @@
         else:
             both = coarse_dot(jnp.concatenate([x, t], axis=0), blocks(turn))
             x, t = both[:rank], both[rank:]
-    x = x + coarse_dot(x, blocks(eye - t))
     for _ in range(2):
         x = x + coarse_dot(x, blocks(eye - dot(a, blocks(x))))
     inverses = blocks(x)
@@ -175,9 +174,10 @@
             for h in range(2):
                 slot = slots[part * 2 * count + 2 * i + h]
                 acc_scr[pl.ds(pl.multiple_of((me ^ slot) * each, each), each), :] = acc[8 * h:8 * h + 8]
-    ones = jnp.ones((8, size), jnp.float32)
-    sums = lax.dot_general(
-        ones, acc_scr[...], (((1,), (1,)), ((), ())), precision=HIGHEST, preferred_element_type=jnp.float32
+    ones = jnp.ones((8, size), jnp.bfloat16)
+    sums = sum(
+        lax.dot_general(ones, part, (((1,), (1,)), ((), ())), preferred_element_type=jnp.float32)
+        for part in split(acc_scr[...], 3)
     )
     o_ref[...] = sums[0:1] * (1.0 / rank)
 
@@ -192,22 +192,24 @@
     moment, example = project(train_inputs, train_grads, proj_in, proj_out)
     far, near = steps[-1], steps[-2]
     slots = [0, far, near, far ^ near]
-    pieces = [query_grads] + [swap(query_grads, step) for step in slots[1:]]
-    moment, early = lax.optimization_barrier((moment, pieces[:2]))
-    sums, order = [moment], steps[:2] + steps[:1:-1]
+    before = {i: swap(query_grads, slots[i]) for i in (1, 3)}
+    first = 1
+    moment, before[first], own = lax.optimization_barrier((moment, before[first], query_grads))
+    sums, order = [moment], steps
     for step in order[:-1]:
         sums.append(sums[-1] + swap(sums[-1], step))
     moment, moment_far = sums[-1], swap(sums[-1], order[-1])
 
     def beside(k, value):
-        return lax.optimization_barrier((sums[k], value))[1]
-
-    pieces = early + [beside(1, piece) for piece in pieces[2:]]
-    queries = jnp.concatenate(pieces[:2], axis=0)
-    received = jnp.concatenate(pieces[2:], axis=0)
+        return value if k is None else lax.optimization_barrier((sums[k], value))[1]
+
+    for i, k in ((2, 0),):
+        before[i] = swap(beside(k, query_grads), slots[i])
+    queries = jnp.concatenate([own, before[1]], axis=0)
+    received = jnp.concatenate([before[2], before[3]], axis=0)
     for step in steps[-3::-1]:
         queries = jnp.concatenate([queries, received], axis=0)
-        received = swap(beside(1, queries) if step == steps[1] else queries, step)
+        received = swap(beside({steps[1]: 1, steps[0]: None}.get(step), queries), step)
         slots = slots + [slot ^ step for slot in slots]
     flat = pl.pallas_call(
         functools.partial(invert_kernel, rank, train_inputs.shape[0] * n),

time: 28.7 us -> 28.3 us (0.986)
  waiting for transfers between devices: 8.2 us -> 7.27 us
  starting transfers between devices: 11.2 us -> 11.9 us
    ppermute x9, waiting for transfers between devices: 8.2 us -> 7.27 us  [swap(): return lax.ppermute(value, 'dp', [(i, i ^ step) for i in range(n)])]
    ppermute x9, starting transfers between devices: 11.2 us -> 11.9 us  [swap(): return lax.ppermute(value, 'dp', [(i, i ^ step) for i in range(n)])]
  transfers between devices with their start and end apart: 9 -> 9, of which waited for: 4 -> 5; matrix products, arithmetic and copies ran while one was open for 0% -> 0% of each run, Pallas kernels for 28% -> 28%
where the time goes in v4:
time: 28.3 us; the launch traced here: 28.2 us
  starting transfers between devices  11.9 us (42%)
  Pallas kernels  8.81 us (31%)
  waiting for transfers between devices  7.27 us (26%)
    ppermute x9, starting transfers between devices, swap(): return lax.ppermute(value, 'dp', [(i, i ^ step) for i in range(n)])  11.9 us
    ppermute x9, waiting for transfers between devices, swap(): return lax.ppermute(value, 'dp', [(i, i ^ step) for i in range(n)])  7.27 us
    pallas_call x1, Pallas kernels, project(): pl.pallas_call(functools.partial(project_kernel, rank, chunk), out_shape=...  5.79 us
    pallas_call x1, Pallas kernels, body(): pl.pallas_call(functools.partial(invert_kernel, rank, train_inputs.shape[...  2.11 us
    pallas_call x1, Pallas kernels, body(): pl.pallas_call(functools.partial(score_kernel, rank, slots), out_shape=ja...  0.92 us
  transfers between devices with their start and end apart: 9, of which 5 were waited for; matrix products, arithmetic and copies ran while one was open for 0% of the time, Pallas kernels for 28%

profile of v4, /device:TPU:0, one launch (start us, length us, event | category | flops | bytes accessed | tf_op | source)
XLA Modules:
  0.0 28.2 jit_solution(15708562408868975244)
XLA Ops:
  0.0 0.0 copy-start
  0.0 4.0 %collective-permute-start = (bf16[8,4096]{1,0:T(8,128)(2,1)}, bf16[8,4096]{1,0:T(8,128)(2,1)S(1)}, u32[]{:S(2)}, u32[]{:S(2)}) collective-permute-start(bf16[8,4096]{1,0:T(8,128)(2,1)} %param.9), channel_id=1, source_target_pairs={{0,8},{1,9},{2,10},{3,11},{4,12},{5,13},{6,14},{7,15},{8,0},{9,1},... | collective-permute-start | bytes 196616 | tf_op jit(solution)/shard_map/ppermute | solution.py:190
  4.0 1.3 %collective-permute-start.6 = (bf16[8,4096]{1,0:T(8,128)(2,1)}, bf16[8,4096]{1,0:T(8,128)(2,1)S(1)}, u32[]{:S(2)}, u32[]{:S(2)}) collective-permute-start(bf16[8,4096]{1,0:T(8,128)(2,1)} %param.9), channel_id=1, source_target_pairs={{0,12},{1,13},{2,14},{3,15},{4,8},{5,9},{6,10},{7,11},{8,4},{9,5},... | collective-permute-start | bytes 196616 | tf_op jit(solution)/shard_map/ppermute | solution.py:190
  5.4 5.8 %project.1 = (f32[64,128]{1,0:T(8,128)S(1)}, f32[64,128]{1,0:T(8,128)S(1)}) custom-call(bf16[256,4096]{1,0:T(8,128)(2,1)} %x_hbm.1, bf16[256,14336]{1,0:T(8,128)(2,1)} %g_hbm.1, bf16[64,4096]{1,0:T(8,128)(2,1)} %pin_hbm.1, bf16[64,14336]{1,0:T(8,128)(2,1)} %pout_hbm.1), custom_call_target="tpu_custom_call" | custom-call | flops 603979776 | bytes 11796480 | tf_op jit(solution)/shard_map/project/pallas_call | solution.py:67
  11.2 0.0 collective-permute-done
  11.2 0.1 collective-permute-start.1
  11.3 0.0 copy-done
  11.3 0.3 %collective-permute-start.5 = (bf16[8,4096]{1,0:T(8,128)(2,1)S(1)}, bf16[8,4096]{1,0:T(8,128)(2,1)S(1)}, u32[]{:S(2)}, u32[]{:S(2)}) collective-permute-start(bf16[8,4096]{1,0:T(8,128)(2,1)S(1)} %copy-done), channel_id=1, source_target_pairs={{0,4},{1,5},{2,6},{3,7},{4,0},{5,1},{6,2},{7,3},{8,12},{9,13},{10,... | collective-permute-start | bytes 196616 | tf_op jit(solution)/shard_map/ppermute | solution.py:190
  11.6 0.9 %collective-permute-done.1 = f32[64,128]{1,0:T(8,128)S(1)} collective-permute-done((f32[64,128]{1,0:T(8,128)S(1)}, f32[64,128]{1,0:T(8,128)S(1)}, u32[]{:S(2)}, u32[]{:S(2)}) %collective-permute-start.1) | collective-permute-done | bytes 32800 | tf_op jit(solution)/shard_map/ppermute | solution.py:190
  12.5 1.5 %collective-permute-start.2 = (f32[64,128]{1,0:T(8,128)S(1)}, f32[64,128]{1,0:T(8,128)S(1)}, u32[]{:S(2)}, u32[]{:S(2)}) collective-permute-start(f32[64,128]{1,0:T(8,128)S(1)} %add.9), channel_id=1, source_target_pairs={{0,2},{1,3},{2,0},{3,1},{4,6},{5,7},{6,4},{7,5},{8,10},{9,11},{10,... | collective-permute-start | bytes 98312 | tf_op jit(solution)/shard_map/ppermute | solution.py:190
  14.0 2.4 %collective-permute-done.2 = f32[64,128]{1,0:T(8,128)S(1)} collective-permute-done((f32[64,128]{1,0:T(8,128)S(1)}, f32[64,128]{1,0:T(8,128)S(1)}, u32[]{:S(2)}, u32[]{:S(2)}) %collective-permute-start.2) | collective-permute-done | bytes 32800 | tf_op jit(solution)/shard_map/ppermute | solution.py:190
  16.4 1.0 %collective-permute-start.3 = (f32[64,128]{1,0:T(8,128)S(1)}, f32[64,128]{1,0:T(8,128)S(1)}, u32[]{:S(2)}, u32[]{:S(2)}) collective-permute-start(f32[64,128]{1,0:T(8,128)S(1)} %add.10), channel_id=1, source_target_pairs={{0,4},{1,5},{2,6},{3,7},{4,0},{5,1},{6,2},{7,3},{8,12},{9,13},{10,... | collective-permute-start | bytes 98312 | tf_op jit(solution)/shard_map/ppermute | solution.py:190
  17.4 0.0 collective-permute-done.6
  17.4 0.0 collective-permute-done.5
  17.4 1.6 %collective-permute-start.7 = (bf16[32,4096]{1,0:T(8,128)(2,1)S(1)}, bf16[32,4096]{1,0:T(8,128)(2,1)S(1)}, u32[]{:S(2)}, u32[]{:S(2)}) collective-permute-start(bf16[32,4096]{1,0:T(8,128)(2,1)S(1)} %pad_maximum_fusion), channel_id=1, source_target_pairs={{0,2},{1,3},{2,0},{3,1},{4,6},{5,7},{6,4},{7,5},{8,10},{9,11},{10,... | collective-permute-start | bytes 786440 | tf_op jit(solution)/shard_map/ppermute | solution.py:190
  19.0 1.3 %collective-permute-done.3 = f32[64,128]{1,0:T(8,128)S(1)} collective-permute-done((f32[64,128]{1,0:T(8,128)S(1)}, f32[64,128]{1,0:T(8,128)S(1)}, u32[]{:S(2)}, u32[]{:S(2)}) %collective-permute-start.3) | collective-permute-done | bytes 32800 | tf_op jit(solution)/shard_map/ppermute | solution.py:190
  20.3 2.0 %collective-permute-start.4 = (f32[64,128]{1,0:T(8,128)S(1)}, f32[64,128]{1,0:T(8,128)S(1)}, u32[]{:S(2)}, u32[]{:S(2)}) collective-permute-start(f32[64,128]{1,0:T(8,128)S(1)} %add.11.m_ref), channel_id=1, source_target_pairs={{0,8},{1,9},{2,10},{3,11},{4,12},{5,13},{6,14},{7,15},{8,0},{9,1},... | collective-permute-start | bytes 98312 | tf_op jit(solution)/shard_map/ppermute | solution.py:190
  22.3 2.1 %collective-permute-done.7 = bf16[32,4096]{1,0:T(8,128)(2,1)S(1)} collective-permute-done((bf16[32,4096]{1,0:T(8,128)(2,1)S(1)}, bf16[32,4096]{1,0:T(8,128)(2,1)S(1)}, u32[]{:S(2)}, u32[]{:S(2)}) %collective-permute-start.7) | collective-permute-done | bytes 262176 | tf_op jit(solution)/shard_map/ppermute | solution.py:190
  24.5 0.1 collective-permute-start.8
  24.6 0.6 %collective-permute-done.4.mr_ref = f32[64,128]{1,0:T(8,128)S(1)} collective-permute-done((f32[64,128]{1,0:T(8,128)S(1)}, f32[64,128]{1,0:T(8,128)S(1)}, u32[]{:S(2)}, u32[]{:S(2)}) %collective-permute-start.4) | collective-permute-done | bytes 32800 | tf_op jit(solution)/shard_map/ppermute | solution.py:190
  25.1 2.1 %invert.1.flat_ref = f32[32,128]{1,0:T(8,128)S(1)} custom-call(f32[64,128]{1,0:T(8,128)S(1)} %add.11.m_ref, f32[64,128]{1,0:T(8,128)S(1)} %collective-permute-done.4.mr_ref, f32[64,128]{1,0:T(8,128)S(1)} %get-tuple-element.14.e_ref), custom_call_target="tpu_custom_call" | custom-call | flops 99999997952 | bytes 100000 | tf_op jit(solution)/shard_map/invert/pallas_call | solution.py:214
  27.2 0.0 collective-permute-done.8.qb_ref
  27.2 0.9 %score.1 = f32[1,128]{1,0:T(1,128)} custom-call(f32[32,128]{1,0:T(8,128)S(1)} %invert.1.flat_ref, bf16[64,4096]{1,0:T(8,128)(2,1)S(1)} %constant_dynamic-update-slice_fusion.qa_ref, bf16[64,4096]{1,0:T(8,128)(2,1)S(1)} %collective-permute-done.8.qb_ref), custom_call_target="tpu_custom_call" | custom-call | tf_op jit(solution)/shard_map/score/pallas_call | solution.py:225
  (9 shorter events, 0.1 us)
Async XLA Ops:
  0.0 11.3 %copy-start = (bf16[8,4096]{1,0:T(8,128)(2,1)S(1)}, bf16[8,4096]{1,0:T(8,128)(2,1)}, u32[]{:S(2)}) copy-start(bf16[8,4096]{1,0:T(8,128)(2,1)} %param.9) | copy-start | bytes 196612
  0.0 11.2 %collective-permute-start = (bf16[8,4096]{1,0:T(8,128)(2,1)}, bf16[8,4096]{1,0:T(8,128)(2,1)S(1)}, u32[]{:S(2)}, u32[]{:S(2)}) collective-permute-start(bf16[8,4096]{1,0:T(8,128)(2,1)} %param.9), channel_id=1, source_target_pairs={{0,8},{1,9},{2,10},{3,11},{4,12},{5,13},{6,14},{7,15},{8,0},{9,1},... | collective-permute-start | bytes 196616 | tf_op jit(solution)/shard_map/ppermute | solution.py:190
  4.0 13.3 %collective-permute-start.6 = (bf16[8,4096]{1,0:T(8,128)(2,1)}, bf16[8,4096]{1,0:T(8,128)(2,1)S(1)}, u32[]{:S(2)}, u32[]{:S(2)}) collective-permute-start(bf16[8,4096]{1,0:T(8,128)(2,1)} %param.9), channel_id=1, source_target_pairs={{0,12},{1,13},{2,14},{3,15},{4,8},{5,9},{6,10},{7,11},{8,4},{9,5},... | collective-permute-start | bytes 196616 | tf_op jit(solution)/shard_map/ppermute | solution.py:190
  11.2 1.3 %collective-permute-start.1 = (f32[64,128]{1,0:T(8,128)S(1)}, f32[64,128]{1,0:T(8,128)S(1)}, u32[]{:S(2)}, u32[]{:S(2)}) collective-permute-start(f32[64,128]{1,0:T(8,128)S(1)} %get-tuple-element.13), channel_id=1, source_target_pairs={{0,1},{1,0},{2,3},{3,2},{4,5},{5,4},{6,7},{7,6},{8,9},{9,8},{10,11... | collective-permute-start | bytes 98312 | tf_op jit(solution)/shard_map/ppermute | solution.py:190
  11.3 6.1 %collective-permute-start.5 = (bf16[8,4096]{1,0:T(8,128)(2,1)S(1)}, bf16[8,4096]{1,0:T(8,128)(2,1)S(1)}, u32[]{:S(2)}, u32[]{:S(2)}) collective-permute-start(bf16[8,4096]{1,0:T(8,128)(2,1)S(1)} %copy-done), channel_id=1, source_target_pairs={{0,4},{1,5},{2,6},{3,7},{4,0},{5,1},{6,2},{7,3},{8,12},{9,13},{10,... | collective-permute-start | bytes 196616 | tf_op jit(solution)/shard_map/ppermute | solution.py:190
  12.5 3.9 %collective-permute-start.2 = (f32[64,128]{1,0:T(8,128)S(1)}, f32[64,128]{1,0:T(8,128)S(1)}, u32[]{:S(2)}, u32[]{:S(2)}) collective-permute-start(f32[64,128]{1,0:T(8,128)S(1)} %add.9), channel_id=1, source_target_pairs={{0,2},{1,3},{2,0},{3,1},{4,6},{5,7},{6,4},{7,5},{8,10},{9,11},{10,... | collective-permute-start | bytes 98312 | tf_op jit(solution)/shard_map/ppermute | solution.py:190
  16.4 3.9 %collective-permute-start.3 = (f32[64,128]{1,0:T(8,128)S(1)}, f32[64,128]{1,0:T(8,128)S(1)}, u32[]{:S(2)}, u32[]{:S(2)}) collective-permute-start(f32[64,128]{1,0:T(8,128)S(1)} %add.10), channel_id=1, source_target_pairs={{0,4},{1,5},{2,6},{3,7},{4,0},{5,1},{6,2},{7,3},{8,12},{9,13},{10,... | collective-permute-start | bytes 98312 | tf_op jit(solution)/shard_map/ppermute | solution.py:190
  17.4 7.1 %collective-permute-start.7 = (bf16[32,4096]{1,0:T(8,128)(2,1)S(1)}, bf16[32,4096]{1,0:T(8,128)(2,1)S(1)}, u32[]{:S(2)}, u32[]{:S(2)}) collective-permute-start(bf16[32,4096]{1,0:T(8,128)(2,1)S(1)} %pad_maximum_fusion), channel_id=1, source_target_pairs={{0,2},{1,3},{2,0},{3,1},{4,6},{5,7},{6,4},{7,5},{8,10},{9,11},{10,... | collective-permute-start | bytes 786440 | tf_op jit(solution)/shard_map/ppermute | solution.py:190
  20.3 4.8 %collective-permute-start.4 = (f32[64,128]{1,0:T(8,128)S(1)}, f32[64,128]{1,0:T(8,128)S(1)}, u32[]{:S(2)}, u32[]{:S(2)}) collective-permute-start(f32[64,128]{1,0:T(8,128)S(1)} %add.11.m_ref), channel_id=1, source_target_pairs={{0,8},{1,9},{2,10},{3,11},{4,12},{5,13},{6,14},{7,15},{8,0},{9,1},... | collective-permute-start | bytes 98312 | tf_op jit(solution)/shard_map/ppermute | solution.py:190
  24.5 2.8 %collective-permute-start.8 = (bf16[64,4096]{1,0:T(8,128)(2,1)S(1)}, bf16[64,4096]{1,0:T(8,128)(2,1)S(1)}, u32[]{:S(2)}, u32[]{:S(2)}) collective-permute-start(bf16[64,4096]{1,0:T(8,128)(2,1)S(1)} %constant_dynamic-update-slice_fusion.qa_ref), channel_id=1, source_target_pairs={{0,1},{1,0},{2,3},{3,2},{4,5},{5,4},{6,7},{7,6},{8,9},{9,8},{10,11... | collective-permute-start | bytes 1572872 | tf_op jit(solution)/shard_map/ppermute | solution.py:190

commit v5 on v4

--- a/solution.py
+++ b/solution.py
@@ -205,11 +205,17 @@
 
     for i, k in ((2, 0),):
         before[i] = swap(beside(k, query_grads), slots[i])
-    queries = jnp.concatenate([own, before[1]], axis=0)
-    received = jnp.concatenate([before[2], before[3]], axis=0)
-    for step in steps[-3::-1]:
-        queries = jnp.concatenate([queries, received], axis=0)
-        received = swap(beside({steps[1]: 1, steps[0]: None}.get(step), queries), step)
+    near_half = jnp.concatenate([own, before[1]], axis=0)
+    far_half = jnp.concatenate([before[2], before[3]], axis=0)
+    for step in steps[-3:1:-1]:
+        near_half, far_half = jnp.concatenate([near_half, far_half], axis=0), jnp.concatenate(
+            [swap(near_half, step), swap(far_half, step)], axis=0
+        )
+        slots = slots + [slot ^ step for slot in slots]
+    halves = (near_half, far_half, swap(beside(0, near_half), steps[1]), swap(beside(1, far_half), steps[1]))
+    queries = jnp.concatenate(halves, axis=0)
+    received = swap(queries, steps[0])
+    for step in steps[1::-1]:
         slots = slots + [slot ^ step for slot in slots]
     flat = pl.pallas_call(
         functools.partial(invert_kernel, rank, train_inputs.shape[0] * n),

time: 28.3 us -> 28.3 us (level)
  starting transfers between devices: 11.9 us -> 12.8 us
  waiting for transfers between devices: 7.27 us -> 6.4 us
    ppermute x9 -> x10, waiting for transfers between devices: 7.27 us -> 6.4 us  [swap(): return lax.ppermute(value, 'dp', [(i, i ^ step) for i in range(n)])]
    ppermute x9 -> x10, starting transfers between devices: 11.9 us -> 12.8 us  [swap(): return lax.ppermute(value, 'dp', [(i, i ^ step) for i in range(n)])]
  transfers between devices with their start and end apart: 9 -> 10, of which waited for: 5 -> 5; matrix products, arithmetic and copies ran while one was open for 0% -> 0% of each run, Pallas kernels for 28% -> 28%
where the time goes in v5:
time: 28.3 us; the launch traced here: 28.2 us
  starting transfers between devices  12.8 us (45%)
  Pallas kernels  8.81 us (31%)
  waiting for transfers between devices  6.4 us (23%)
    ppermute x10, starting transfers between devices, swap(): return lax.ppermute(value, 'dp', [(i, i ^ step) for i in range(n)])  12.8 us
    ppermute x10, waiting for transfers between devices, swap(): return lax.ppermute(value, 'dp', [(i, i ^ step) for i in range(n)])  6.4 us
    pallas_call x1, Pallas kernels, project(): pl.pallas_call(functools.partial(project_kernel, rank, chunk), out_shape=...  5.79 us
    pallas_call x1, Pallas kernels, body(): pl.pallas_call(functools.partial(invert_kernel, rank, train_inputs.shape[...  2.11 us
    pallas_call x1, Pallas kernels, body(): pl.pallas_call(functools.partial(score_kernel, rank, slots), out_shape=ja...  0.92 us
  transfers between devices with their start and end apart: 10, of which 5 were waited for; matrix products, arithmetic and copies ran while one was open for 0% of the time, Pallas kernels for 28%

profile of v5, /device:TPU:0, one launch (start us, length us, event | category | flops | bytes accessed | tf_op | source)
XLA Modules:
  0.0 28.2 jit_solution(9108125081126032185)
XLA Ops:
  0.0 0.0 copy-start
  0.0 4.0 %collective-permute-start = (bf16[8,4096]{1,0:T(8,128)(2,1)}, bf16[8,4096]{1,0:T(8,128)(2,1)S(1)}, u32[]{:S(2)}, u32[]{:S(2)}) collective-permute-start(bf16[8,4096]{1,0:T(8,128)(2,1)} %param.9), channel_id=1, source_target_pairs={{0,8},{1,9},{2,10},{3,11},{4,12},{5,13},{6,14},{7,15},{8,0},{9,1},... | collective-permute-start | bytes 196616 | tf_op jit(solution)/shard_map/ppermute | solution.py:190
  4.0 1.3 %collective-permute-start.6 = (bf16[8,4096]{1,0:T(8,128)(2,1)}, bf16[8,4096]{1,0:T(8,128)(2,1)S(1)}, u32[]{:S(2)}, u32[]{:S(2)}) collective-permute-start(bf16[8,4096]{1,0:T(8,128)(2,1)} %param.9), channel_id=1, source_target_pairs={{0,12},{1,13},{2,14},{3,15},{4,8},{5,9},{6,10},{7,11},{8,4},{9,5},... | collective-permute-start | bytes 196616 | tf_op jit(solution)/shard_map/ppermute | solution.py:190
  5.4 5.8 %project.1 = (f32[64,128]{1,0:T(8,128)S(1)}, f32[64,128]{1,0:T(8,128)S(1)}) custom-call(bf16[256,4096]{1,0:T(8,128)(2,1)} %x_hbm.1, bf16[256,14336]{1,0:T(8,128)(2,1)} %g_hbm.1, bf16[64,4096]{1,0:T(8,128)(2,1)} %pin_hbm.1, bf16[64,14336]{1,0:T(8,128)(2,1)} %pout_hbm.1), custom_call_target="tpu_custom_call" | custom-call | flops 603979776 | bytes 11796480 | tf_op jit(solution)/shard_map/project/pallas_call | solution.py:67
  11.2 0.0 collective-permute-done
  11.2 0.1 collective-permute-start.1
  11.3 0.0 copy-done
  11.3 0.3 %collective-permute-start.5 = (bf16[8,4096]{1,0:T(8,128)(2,1)S(1)}, bf16[8,4096]{1,0:T(8,128)(2,1)S(1)}, u32[]{:S(2)}, u32[]{:S(2)}) collective-permute-start(bf16[8,4096]{1,0:T(8,128)(2,1)S(1)} %copy-done), channel_id=1, source_target_pairs={{0,4},{1,5},{2,6},{3,7},{4,0},{5,1},{6,2},{7,3},{8,12},{9,13},{10,... | collective-permute-start | bytes 196616 | tf_op jit(solution)/shard_map/ppermute | solution.py:190
  11.6 0.9 %collective-permute-done.1 = f32[64,128]{1,0:T(8,128)S(1)} collective-permute-done((f32[64,128]{1,0:T(8,128)S(1)}, f32[64,128]{1,0:T(8,128)S(1)}, u32[]{:S(2)}, u32[]{:S(2)}) %collective-permute-start.1) | collective-permute-done | bytes 32800 | tf_op jit(solution)/shard_map/ppermute | solution.py:190
  12.5 1.5 %collective-permute-start.2 = (f32[64,128]{1,0:T(8,128)S(1)}, f32[64,128]{1,0:T(8,128)S(1)}, u32[]{:S(2)}, u32[]{:S(2)}) collective-permute-start(f32[64,128]{1,0:T(8,128)S(1)} %add.9), channel_id=1, source_target_pairs={{0,2},{1,3},{2,0},{3,1},{4,6},{5,7},{6,4},{7,5},{8,10},{9,11},{10,... | collective-permute-start | bytes 98312 | tf_op jit(solution)/shard_map/ppermute | solution.py:190
  14.0 0.5 %collective-permute-start.7 = (bf16[16,4096]{1,0:T(8,128)(2,1)S(1)}, bf16[16,4096]{1,0:T(8,128)(2,1)S(1)}, u32[]{:S(2)}, u32[]{:S(2)}) collective-permute-start(bf16[16,4096]{1,0:T(8,128)(2,1)S(1)} %pad_maximum_fusion), channel_id=1, source_target_pairs={{0,2},{1,3},{2,0},{3,1},{4,6},{5,7},{6,4},{7,5},{8,10},{9,11},{10,... | collective-permute-start | bytes 393224 | tf_op jit(solution)/shard_map/ppermute | solution.py:190
  14.5 1.9 %collective-permute-done.2 = f32[64,128]{1,0:T(8,128)S(1)} collective-permute-done((f32[64,128]{1,0:T(8,128)S(1)}, f32[64,128]{1,0:T(8,128)S(1)}, u32[]{:S(2)}, u32[]{:S(2)}) %collective-permute-start.2) | collective-permute-done | bytes 32800 | tf_op jit(solution)/shard_map/ppermute | solution.py:190
  16.4 1.0 %collective-permute-start.3 = (f32[64,128]{1,0:T(8,128)S(1)}, f32[64,128]{1,0:T(8,128)S(1)}, u32[]{:S(2)}, u32[]{:S(2)}) collective-permute-start(f32[64,128]{1,0:T(8,128)S(1)} %add.10), channel_id=1, source_target_pairs={{0,4},{1,5},{2,6},{3,7},{4,0},{5,1},{6,2},{7,3},{8,12},{9,13},{10,... | collective-permute-start | bytes 98312 | tf_op jit(solution)/shard_map/ppermute | solution.py:190
  17.4 0.0 collective-permute-done.6
  17.4 0.0 collective-permute-done.5
  17.4 1.9 %collective-permute-start.8 = (bf16[16,4096]{1,0:T(8,128)(2,1)S(1)}, bf16[16,4096]{1,0:T(8,128)(2,1)S(1)}, u32[]{:S(2)}, u32[]{:S(2)}) collective-permute-start(bf16[16,4096]{1,0:T(8,128)(2,1)S(1)} %pad_maximum_fusion.1), channel_id=1, source_target_pairs={{0,2},{1,3},{2,0},{3,1},{4,6},{5,7},{6,4},{7,5},{8,10},{9,11},{10,... | collective-permute-start | bytes 393224 | tf_op jit(solution)/shard_map/ppermute | solution.py:190
  19.3 1.0 %collective-permute-done.3 = f32[64,128]{1,0:T(8,128)S(1)} collective-permute-done((f32[64,128]{1,0:T(8,128)S(1)}, f32[64,128]{1,0:T(8,128)S(1)}, u32[]{:S(2)}, u32[]{:S(2)}) %collective-permute-start.3) | collective-permute-done | bytes 32800 | tf_op jit(solution)/shard_map/ppermute | solution.py:190
  20.3 2.0 %collective-permute-start.4 = (f32[64,128]{1,0:T(8,128)S(1)}, f32[64,128]{1,0:T(8,128)S(1)}, u32[]{:S(2)}, u32[]{:S(2)}) collective-permute-start(f32[64,128]{1,0:T(8,128)S(1)} %add.11.m_ref), channel_id=1, source_target_pairs={{0,8},{1,9},{2,10},{3,11},{4,12},{5,13},{6,14},{7,15},{8,0},{9,1},... | collective-permute-start | bytes 98312 | tf_op jit(solution)/shard_map/ppermute | solution.py:190
  22.3 0.0 collective-permute-done.7
  22.4 0.1 collective-permute-done.8
  22.5 0.1 collective-permute-start.9
  22.6 2.6 %collective-permute-done.4.mr_ref = f32[64,128]{1,0:T(8,128)S(1)} collective-permute-done((f32[64,128]{1,0:T(8,128)S(1)}, f32[64,128]{1,0:T(8,128)S(1)}, u32[]{:S(2)}, u32[]{:S(2)}) %collective-permute-start.4) | collective-permute-done | bytes 32800 | tf_op jit(solution)/shard_map/ppermute | solution.py:190
  25.1 2.1 %invert.1.flat_ref = f32[32,128]{1,0:T(8,128)S(1)} custom-call(f32[64,128]{1,0:T(8,128)S(1)} %add.11.m_ref, f32[64,128]{1,0:T(8,128)S(1)} %collective-permute-done.4.mr_ref, f32[64,128]{1,0:T(8,128)S(1)} %get-tuple-element.15.e_ref), custom_call_target="tpu_custom_call" | custom-call | flops 99999997952 | bytes 100000 | tf_op jit(solution)/shard_map/invert/pallas_call | solution.py:220
  27.2 0.0 collective-permute-done.9.qb_ref
  27.2 0.9 %score.1 = f32[1,128]{1,0:T(1,128)} custom-call(f32[32,128]{1,0:T(8,128)S(1)} %invert.1.flat_ref, bf16[64,4096]{1,0:T(8,128)(2,1)S(1)} %constant_dynamic-update-slice_fusion.qa_ref, bf16[64,4096]{1,0:T(8,128)(2,1)S(1)} %collective-permute-done.9.qb_ref), custom_call_target="tpu_custom_call" | custom-call | tf_op jit(solution)/shard_map/score/pallas_call | solution.py:231
  (11 shorter events, 0.1 us)
Async XLA Ops:
  0.0 11.3 %copy-start = (bf16[8,4096]{1,0:T(8,128)(2,1)S(1)}, bf16[8,4096]{1,0:T(8,128)(2,1)}, u32[]{:S(2)}) copy-start(bf16[8,4096]{1,0:T(8,128)(2,1)} %param.9) | copy-start | bytes 196612
  0.0 11.2 %collective-permute-start = (bf16[8,4096]{1,0:T(8,128)(2,1)}, bf16[8,4096]{1,0:T(8,128)(2,1)S(1)}, u32[]{:S(2)}, u32[]{:S(2)}) collective-permute-start(bf16[8,4096]{1,0:T(8,128)(2,1)} %param.9), channel_id=1, source_target_pairs={{0,8},{1,9},{2,10},{3,11},{4,12},{5,13},{6,14},{7,15},{8,0},{9,1},... | collective-permute-start | bytes 196616 | tf_op jit(solution)/shard_map/ppermute | solution.py:190
  4.0 13.4 %collective-permute-start.6 = (bf16[8,4096]{1,0:T(8,128)(2,1)}, bf16[8,4096]{1,0:T(8,128)(2,1)S(1)}, u32[]{:S(2)}, u32[]{:S(2)}) collective-permute-start(bf16[8,4096]{1,0:T(8,128)(2,1)} %param.9), channel_id=1, source_target_pairs={{0,12},{1,13},{2,14},{3,15},{4,8},{5,9},{6,10},{7,11},{8,4},{9,5},... | collective-permute-start | bytes 196616 | tf_op jit(solution)/shard_map/ppermute | solution.py:190
  11.2 1.3 %collective-permute-start.1 = (f32[64,128]{1,0:T(8,128)S(1)}, f32[64,128]{1,0:T(8,128)S(1)}, u32[]{:S(2)}, u32[]{:S(2)}) collective-permute-start(f32[64,128]{1,0:T(8,128)S(1)} %get-tuple-element.14), channel_id=1, source_target_pairs={{0,1},{1,0},{2,3},{3,2},{4,5},{5,4},{6,7},{7,6},{8,9},{9,8},{10,11... | collective-permute-start | bytes 98312 | tf_op jit(solution)/shard_map/ppermute | solution.py:190
  11.3 6.1 %collective-permute-start.5 = (bf16[8,4096]{1,0:T(8,128)(2,1)S(1)}, bf16[8,4096]{1,0:T(8,128)(2,1)S(1)}, u32[]{:S(2)}, u32[]{:S(2)}) collective-permute-start(bf16[8,4096]{1,0:T(8,128)(2,1)S(1)} %copy-done), channel_id=1, source_target_pairs={{0,4},{1,5},{2,6},{3,7},{4,0},{5,1},{6,2},{7,3},{8,12},{9,13},{10,... | collective-permute-start | bytes 196616 | tf_op jit(solution)/shard_map/ppermute | solution.py:190
  12.5 3.9 %collective-permute-start.2 = (f32[64,128]{1,0:T(8,128)S(1)}, f32[64,128]{1,0:T(8,128)S(1)}, u32[]{:S(2)}, u32[]{:S(2)}) collective-permute-start(f32[64,128]{1,0:T(8,128)S(1)} %add.9), channel_id=1, source_target_pairs={{0,2},{1,3},{2,0},{3,1},{4,6},{5,7},{6,4},{7,5},{8,10},{9,11},{10,... | collective-permute-start | bytes 98312 | tf_op jit(solution)/shard_map/ppermute | solution.py:190
  14.0 8.3 %collective-permute-start.7 = (bf16[16,4096]{1,0:T(8,128)(2,1)S(1)}, bf16[16,4096]{1,0:T(8,128)(2,1)S(1)}, u32[]{:S(2)}, u32[]{:S(2)}) collective-permute-start(bf16[16,4096]{1,0:T(8,128)(2,1)S(1)} %pad_maximum_fusion), channel_id=1, source_target_pairs={{0,2},{1,3},{2,0},{3,1},{4,6},{5,7},{6,4},{7,5},{8,10},{9,11},{10,... | collective-permute-start | bytes 393224 | tf_op jit(solution)/shard_map/ppermute | solution.py:190
  16.4 3.9 %collective-permute-start.3 = (f32[64,128]{1,0:T(8,128)S(1)}, f32[64,128]{1,0:T(8,128)S(1)}, u32[]{:S(2)}, u32[]{:S(2)}) collective-permute-start(f32[64,128]{1,0:T(8,128)S(1)} %add.10), channel_id=1, source_target_pairs={{0,4},{1,5},{2,6},{3,7},{4,0},{5,1},{6,2},{7,3},{8,12},{9,13},{10,... | collective-permute-start | bytes 98312 | tf_op jit(solution)/shard_map/ppermute | solution.py:190
  17.4 5.0 %collective-permute-start.8 = (bf16[16,4096]{1,0:T(8,128)(2,1)S(1)}, bf16[16,4096]{1,0:T(8,128)(2,1)S(1)}, u32[]{:S(2)}, u32[]{:S(2)}) collective-permute-start(bf16[16,4096]{1,0:T(8,128)(2,1)S(1)} %pad_maximum_fusion.1), channel_id=1, source_target_pairs={{0,2},{1,3},{2,0},{3,1},{4,6},{5,7},{6,4},{7,5},{8,10},{9,11},{10,... | collective-permute-start | bytes 393224 | tf_op jit(solution)/shard_map/ppermute | solution.py:190
  20.3 4.8 %collective-permute-start.4 = (f32[64,128]{1,0:T(8,128)S(1)}, f32[64,128]{1,0:T(8,128)S(1)}, u32[]{:S(2)}, u32[]{:S(2)}) collective-permute-start(f32[64,128]{1,0:T(8,128)S(1)} %add.11.m_ref), channel_id=1, source_target_pairs={{0,8},{1,9},{2,10},{3,11},{4,12},{5,13},{6,14},{7,15},{8,0},{9,1},... | collective-permute-start | bytes 98312 | tf_op jit(solution)/shard_map/ppermute | solution.py:190
  22.5 4.8 %collective-permute-start.9 = (bf16[64,4096]{1,0:T(8,128)(2,1)S(1)}, bf16[64,4096]{1,0:T(8,128)(2,1)S(1)}, u32[]{:S(2)}, u32[]{:S(2)}) collective-permute-start(bf16[64,4096]{1,0:T(8,128)(2,1)S(1)} %constant_dynamic-update-slice_fusion.qa_ref), channel_id=1, source_target_pairs={{0,1},{1,0},{2,3},{3,2},{4,5},{5,4},{6,7},{7,6},{8,9},{9,8},{10,11... | collective-permute-start | bytes 1572872 | tf_op jit(solution)/shard_map/ppermute | solution.py:190
